TPU v7x, 32 devices: a whole 2x2x4 slice. The times are simulated.
32 devices in a mesh: dp: 16 (over z, y, x), pipe: 2 (over core).
Axes of the slice: x: 2, y: 2, z: 4, core: 2. Of those that a mesh axis runs over, the one named last changes fastest.
Arguments:
- section_input: bfloat16 [2, 32, 512, 768], P('pipe', 'dp'), may hold values from -6 to 6
- visible_slot: int32 [32, 512], P('dp'), may hold values from 0 to 128, as said below
- image_of_slot: int32 [32, 512], P('dp'), may hold values from 0 to 1, as said below
- qkv_weight: bfloat16 [2, 768, 2304], P('pipe'), may hold values from -0.21875 to 0.21875
- out_weight: bfloat16 [2, 768, 768], P('pipe'), may hold values from -1.25 to 1.25
- up_weight: bfloat16 [2, 768, 3072], P('pipe'), may hold values from -0.21875 to 0.21875
- down_weight: bfloat16 [2, 3072, 768], P('pipe'), may hold values from -0.21875 to 0.21875
- norm_gain: float32 [2, 2, 768], P('pipe'), may hold values from 0.5 to 1.5
- up_bias: float32 [2, 3072], P('pipe'), may hold values from -3 to 3
- vectors: float32 [2, 7, 768], P('pipe'), may hold values from -3 to 3
Outputs:
- results: bfloat16 [2, 32, 512, 768], P('pipe', 'dp')
- qkv_weight_grad: float32 [2, 768, 2304], P('pipe', 'dp')
- out_weight_grad: float32 [2, 768, 768], P('pipe', 'dp')
- up_weight_grad: float32 [2, 768, 3072], P('pipe', 'dp')
- down_weight_grad: float32 [2, 3072, 768], P('pipe', 'dp')
- norm_gain_grad: float32 [2, 2, 768], P('pipe', None, 'dp')
- up_bias_grad: float32 [2, 3072], P('pipe', 'dp')
- vectors_grad: float32 [2, 7, 768], P('pipe', None, 'dp')
Inputs may be any that keep to these rules, and one draw needn't show every extreme that they name: `visible_slot`: in each micro-batch the visible slots carry the places 0, 1, 2, ... in slot order; at least 96 slots are visible, and some micro-batch has exactly 128. `image_of_slot`: each micro-batch holds either one image on all 512 slots (all 0) or two images of 256 consecutive slots numbered 0 and 1; both kinds occur.
All inputs are finite; a program needn't handle non-finite values.
Results may differ from a plain program's by a relative error of at most 0.0095.
Values may be sent and summed in bfloat16 or wider, within the bound.
No kernel may reach another device: no remote copies, remote signals or barrier semaphores. Data moves between devices by JAX's collectives and lax.ppermute only.
A program may use at most 320 MiB of HBM per device.

v0:
```python
import math

import jax
import jax.numpy as jnp
from jax import lax
from jax.sharding import PartitionSpec as P

D = 768
H = 12
HD = 64
S = 512
VIS = 128
MICRO = 2


EPSILON = 1e-06


def swapped(value, axis, stride):
    mask = 2**stride
    pairs = [(source, source ^ mask) for source in range(lax.axis_size(axis))]
    return lax.ppermute(value, axis, pairs)


def layer_norm(inputs, gain_vec, shift_vec):
    row_mean = jnp.mean(inputs, axis=-1, keepdims=True)
    centered = inputs - row_mean
    variance = jnp.mean(centered * centered, axis=-1, keepdims=True)
    return centered * lax.rsqrt(variance + EPSILON) * gain_vec + shift_vec


def exact_gelu(values):
    return jax.nn.gelu(values, approximate=False)


def positions(slot_count, model_width):
    half_width = model_width // 2
    frequency = jnp.exp(
        jnp.arange(half_width, dtype=jnp.float32) * (-math.log(10000.0) / half_width)
    )
    angles = jnp.arange(slot_count, dtype=jnp.float32)[:, None] * frequency[None, :]
    return jnp.concatenate([jnp.sin(angles), jnp.cos(angles)], axis=1)


def split_heads(packed):
    pieces = packed.reshape(packed.shape[0], 3, H, HD)
    return (pieces[:, 0], pieces[:, 1], pieces[:, 2])


def masked_scores(row_block, row_marks, keys_all, group_ids):
    scores = jnp.einsum(
        "qhd,khd->hqk", row_block, keys_all, preferred_element_type=jnp.float32
    ) * HD ** (-0.5)
    return jnp.where((row_marks[:, None] == group_ids[None, :])[None], scores, -1e30)


def attention_forward(queries, keys_all, values, group_ids):
    length_rows = queries.shape[0]
    block_rows = min(512, length_rows)
    block_count = length_rows // block_rows

    def one_block(pieces):
        row_block, row_marks = pieces
        scores = masked_scores(row_block, row_marks, keys_all, group_ids)
        row_top = jnp.max(scores, axis=-1, keepdims=True)
        raised = jnp.exp(scores - row_top)
        totals = jnp.sum(raised, axis=-1, keepdims=True)
        probs = (raised / totals).astype(jnp.bfloat16)
        attended = jnp.einsum("hqk,khd->qhd", probs, values, preferred_element_type=jnp.float32)
        return (attended, (row_top + jnp.log(totals))[..., 0])

    attended, logsum = lax.map(
        one_block,
        (
            queries.reshape(block_count, block_rows, H, HD),
            group_ids.reshape(block_count, block_rows),
        ),
    )
    return (attended.reshape(length_rows, H * HD), logsum)


def attention_backward(queries, keys_all, values, group_ids, logsum, grad_attended):
    length_rows = queries.shape[0]
    block_rows = min(512, length_rows)
    block_count = length_rows // block_rows
    scaling = HD ** (-0.5)

    def one_block(carry, pieces):
        key_acc, value_acc = carry
        row_block, row_marks, row_logs, grad_block = pieces
        scores = masked_scores(row_block, row_marks, keys_all, group_ids)
        probs = jnp.exp(scores - row_logs[..., None])
        value_acc = value_acc + jnp.einsum(
            "hqk,qhd->khd",
            probs.astype(jnp.bfloat16),
            grad_block,
            preferred_element_type=jnp.float32,
        )
        dprobs = jnp.einsum("qhd,khd->hqk", grad_block, values, preferred_element_type=jnp.float32)
        dscores = (probs * (dprobs - jnp.sum(probs * dprobs, axis=-1, keepdims=True))).astype(
            jnp.bfloat16
        )
        drows = (
            jnp.einsum("hqk,khd->qhd", dscores, keys_all, preferred_element_type=jnp.float32)
            * scaling
        )
        key_acc = (
            key_acc
            + jnp.einsum("hqk,qhd->khd", dscores, row_block, preferred_element_type=jnp.float32)
            * scaling
        )
        return ((key_acc, value_acc), drows)

    zeros_keys = jnp.zeros(keys_all.shape, jnp.float32)
    (grad_keys, grad_values), grad_queries = lax.scan(
        one_block,
        (zeros_keys, zeros_keys),
        (
            queries.reshape(block_count, block_rows, H, HD),
            group_ids.reshape(block_count, block_rows),
            logsum,
            grad_attended.reshape(block_count, block_rows, H, HD),
        ),
    )
    return (grad_queries.reshape(length_rows, H, HD), grad_keys, grad_values)


def block_forward(inputs, group_ids, weights):
    w_qkv, w_out, w_up, w_down, gains, hidden_bias, vecs = weights
    normed = layer_norm(inputs, gains[0], vecs[0]).astype(jnp.bfloat16)
    qkv_bias = jnp.concatenate([vecs[1], jnp.zeros_like(vecs[1]), vecs[2]])
    packed = (jnp.dot(normed, w_qkv, preferred_element_type=jnp.float32) + qkv_bias).astype(
        jnp.bfloat16
    )
    queries, keys_all, values = split_heads(packed)
    attended, logsum = attention_forward(queries, keys_all, values, group_ids)
    attended = attended.astype(jnp.bfloat16)
    middle = inputs + jnp.dot(attended, w_out, preferred_element_type=jnp.float32) + vecs[3]
    normed_two = layer_norm(middle, gains[1], vecs[5]).astype(jnp.bfloat16)
    preact = jnp.dot(normed_two, w_up, preferred_element_type=jnp.float32) + hidden_bias
    activated = exact_gelu(preact).astype(jnp.bfloat16)
    output = middle + jnp.dot(activated, w_down, preferred_element_type=jnp.float32) + vecs[6]
    return (output, (normed, packed, attended, logsum, middle, normed_two, preact, activated))


def block_backward(inputs, group_ids, stored, grad_out, weights, accum):
    w_qkv, w_out, w_up, w_down, gains, hidden_bias, vecs = weights
    acc_qkv, acc_out, acc_up, acc_down, acc_gains, acc_ubias, acc_vecs = accum
    normed, packed, attended, logsum, middle, normed_two, preact, activated = stored
    length_rows = inputs.shape[0]
    model_width = H * HD
    grad_feed = grad_out.astype(jnp.bfloat16)
    acc_down = acc_down + jnp.einsum(
        "nf,nd->fd", activated, grad_feed, preferred_element_type=jnp.float32
    )
    grad_dbias = jnp.sum(grad_feed.astype(jnp.float32), axis=0)
    grad_act = jnp.einsum("nd,fd->nf", grad_feed, w_down, preferred_element_type=jnp.float32)
    _, gelu_pull = jax.vjp(exact_gelu, preact)
    grad_pre = gelu_pull(grad_act)[0].astype(jnp.bfloat16)
    acc_up = acc_up + jnp.einsum(
        "nd,nf->df", normed_two, grad_pre, preferred_element_type=jnp.float32
    )
    acc_ubias = acc_ubias + jnp.sum(grad_pre.astype(jnp.float32), axis=0)
    grad_normed_two = jnp.einsum("nf,df->nd", grad_pre, w_up, preferred_element_type=jnp.float32)
    _, second_pull = jax.vjp(layer_norm, middle, gains[1], vecs[5])
    grad_mid_norm, grad_gain_two, grad_shift_two = second_pull(grad_normed_two)
    grad_middle = grad_out + grad_mid_norm
    grad_branch = grad_middle.astype(jnp.bfloat16)
    acc_out = acc_out + jnp.einsum(
        "nd,ne->de", attended, grad_branch, preferred_element_type=jnp.float32
    )
    grad_obias = jnp.sum(grad_branch.astype(jnp.float32), axis=0)
    grad_attended = jnp.einsum(
        "ne,de->nd", grad_branch, w_out, preferred_element_type=jnp.float32
    ).astype(jnp.bfloat16)
    queries, keys_all, values = split_heads(packed)
    grad_queries, grad_keys, grad_values = attention_backward(
        queries, keys_all, values, group_ids, logsum, grad_attended
    )
    grad_packed = (
        jnp.stack([grad_queries, grad_keys, grad_values], axis=1)
        .reshape(length_rows, 3 * model_width)
        .astype(jnp.bfloat16)
    )
    acc_qkv = acc_qkv + jnp.einsum(
        "nd,ne->de", normed, grad_packed, preferred_element_type=jnp.float32
    )
    summed = jnp.sum(grad_packed.astype(jnp.float32), axis=0)
    grad_normed = jnp.einsum("ne,de->nd", grad_packed, w_qkv, preferred_element_type=jnp.float32)
    _, first_pull = jax.vjp(layer_norm, inputs, gains[0], vecs[0])
    grad_inputs, grad_gain, grad_shift = first_pull(grad_normed)
    zero_row = jnp.zeros_like(grad_shift)
    acc_vecs = acc_vecs + jnp.stack(
        [
            grad_shift,
            summed[:model_width],
            summed[2 * model_width :],
            grad_obias,
            zero_row,
            grad_shift_two,
            grad_dbias,
        ]
    )
    acc_gains = acc_gains + jnp.stack([grad_gain, grad_gain_two])
    return (
        grad_middle + grad_inputs,
        (acc_qkv, acc_out, acc_up, acc_down, acc_gains, acc_ubias, acc_vecs),
    )


def on_device(
    section_input,
    visible_slot,
    image_of_slot,
    qkv_weight,
    out_weight,
    up_weight,
    down_weight,
    norm_gain,
    up_bias,
    vectors,
):
    section_index = lax.axis_index("pipe")
    section_data = section_input[0]
    weights = (
        qkv_weight[0],
        out_weight[0],
        up_weight[0],
        down_weight[0],
        norm_gain[0],
        up_bias[0],
        vectors[0],
    )
    vecs = vectors[0]
    pos_table = positions(S, D)
    columns = jnp.arange(VIS)

    def layout(micro_index):
        slot_map = visible_slot[micro_index]
        slot_hit = slot_map[:, None] == columns[None, :]
        images = image_of_slot[micro_index]
        group_ids = jnp.where(
            jnp.any(slot_hit, axis=0), jnp.sum(jnp.where(slot_hit, images[:, None], 0), axis=0), -1
        )
        masked = (slot_map == VIS).astype(jnp.float32)[:, None]
        return (slot_map, slot_hit.astype(jnp.bfloat16), group_ids, masked, images)

    def encoder_forward(micro_index):
        slot_map, selector, group_ids, masked, images = layout(micro_index)
        entry_rows = (
            jnp.einsum(
                "sv,sd->vd", selector, section_data[micro_index], preferred_element_type=jnp.float32
            )
            + vecs[4]
        )
        encoded, stored = block_forward(entry_rows, group_ids, weights)
        return (entry_rows, group_ids, slot_map, encoded, stored)

    def encoder_backward(micro_index, received, accum):
        entry_rows, group_ids, slot_map, encoded, stored = encoder_forward(micro_index)
        grad_entry, accum = block_backward(
            entry_rows, group_ids, stored, received.astype(jnp.float32), weights, accum
        )
        padded = jnp.concatenate([grad_entry, jnp.zeros((1, D), jnp.float32)], axis=0)
        grad_rows = padded[slot_map].astype(jnp.bfloat16)
        grad_vecs = accum[6].at[4].add(jnp.sum(grad_entry, axis=0))
        return (grad_rows, accum[:6] + (grad_vecs,))

    def decoder_step(micro_index, received, accum):
        slot_map, selector, group_ids, masked, images = layout(micro_index)
        dec_input = (
            jnp.einsum("sv,vd->sd", selector, received, preferred_element_type=jnp.float32)
            + masked * vecs[4]
            + pos_table
        )
        decoded, stored = block_forward(dec_input, images, weights)
        grad_input, accum = block_backward(
            dec_input, images, stored, section_data[micro_index].astype(jnp.float32), weights, accum
        )
        grad_vecs = accum[6].at[4].add(jnp.sum(masked * grad_input, axis=0))
        returned = jnp.einsum(
            "sv,sd->vd",
            selector,
            grad_input.astype(jnp.bfloat16),
            preferred_element_type=jnp.float32,
        ).astype(jnp.bfloat16)
        return (returned, decoded.astype(jnp.bfloat16), accum[:6] + (grad_vecs,))

    zeros_send = jnp.zeros((VIS, D), jnp.bfloat16)
    zeros_row = jnp.zeros((S, D), jnp.bfloat16)
    received = zeros_send
    grad_sums = tuple((jnp.zeros(weight.shape, jnp.float32) for weight in weights))
    out_rows = []
    for tick_index in range(MICRO + 2):

        def first_section(operands):
            incoming, accum = operands
            outgoing = zeros_send
            out_row = zeros_row
            if tick_index < MICRO:
                outgoing = encoder_forward(tick_index)[3].astype(jnp.bfloat16)
            if tick_index >= 2:
                out_row, accum = encoder_backward(tick_index - 2, incoming, accum)
            return (outgoing, out_row, accum)

        def second_section(operands):
            incoming, accum = operands
            if 1 <= tick_index <= MICRO:
                return decoder_step(tick_index - 1, incoming, accum)
            return (zeros_send, zeros_row, accum)

        outgoing, out_row, grad_sums = lax.cond(
            section_index == 0, first_section, second_section, (received, grad_sums)
        )
        out_rows.append(out_row)
        if tick_index <= MICRO:
            received = swapped(outgoing, "pipe", 0)
    grad_sums = (
        lax.psum_scatter(grad_sums[0], "dp", scatter_dimension=0, tiled=True),
        lax.psum_scatter(grad_sums[1], "dp", scatter_dimension=0, tiled=True),
        lax.psum_scatter(grad_sums[2], "dp", scatter_dimension=0, tiled=True),
        lax.psum_scatter(grad_sums[3], "dp", scatter_dimension=0, tiled=True),
        lax.psum_scatter(grad_sums[4], "dp", scatter_dimension=1, tiled=True),
        lax.psum_scatter(grad_sums[5], "dp", scatter_dimension=0, tiled=True),
        lax.psum_scatter(grad_sums[6], "dp", scatter_dimension=1, tiled=True),
    )
    results = jnp.stack(
        [
            jnp.where(section_index == 0, out_rows[micro + 2], out_rows[micro + 1])
            for micro in range(MICRO)
        ]
    )
    return (
        results[None],
        grad_sums[0][None],
        grad_sums[1][None],
        grad_sums[2][None],
        grad_sums[3][None],
        grad_sums[4][None],
        grad_sums[5][None],
        grad_sums[6][None],
    )


def solution(mesh):
    in_specs = (
        P("pipe", "dp", None, None),
        P("dp", None),
        P("dp", None),
        P("pipe", None, None),
        P("pipe", None, None),
        P("pipe", None, None),
        P("pipe", None, None),
        P("pipe", None, None),
        P("pipe", None),
        P("pipe", None, None),
    )
    out_specs = (
        P("pipe", "dp", None, None),
        P("pipe", "dp", None),
        P("pipe", "dp", None),
        P("pipe", "dp", None),
        P("pipe", "dp", None),
        P("pipe", None, "dp"),
        P("pipe", "dp"),
        P("pipe", None, "dp"),
    )
    return jax.shard_map(
        on_device, mesh=mesh, in_specs=in_specs, out_specs=out_specs, check_vma=False
    )
```

profile of v0, /device:TPU:0, one launch (start us, length us, event | category | flops | bytes accessed | tf_op | source)
XLA Modules:
  0.0 1305.4 jit_solution(3859999228704196685)
XLA Ops:
  7.2 1.3 copy.172
  9.1 20.4 %conditional.7 = (bf16[128,768]{1,0:T(8,128)(2,1)}) conditional(s32[]{:T(128)} %convert_element_type.367, () %tuple.87, (s32[2,512]{1,0:T(2,128)}, s32[128]{0:T(128)}, bf16[2,512,768]{2,1,0:T(8,128)(2,1)}, f32[7,768]{1,0:T(8,128)}, f32[2,768]{1,0:T(2,128)}, /*index=5*/bf16[768,2304]{1,0:T(8,128)(2,1)}, s32[2,512]{1,0:T(2,128)}, ...), branch_computations={%region_0.0_spmd, %region_1.10_spmd} | conditional | flops 2019285376 | bytes 28393312 | solution.py:312
  10.8 1.7 fusion.363
  12.8 2.7 fusion.1
  20.3 9.2 fusion.17
  29.5 2.8 fusion.346
  33.6 52.1 %conditional.8 = (bf16[128,768]{1,0:T(8,128)(2,1)S(1)}, bf16[512,768]{1,0:T(8,128)(2,1)S(1)}, f32[768,2304]{1,0:T(8,128)}, f32[768,768]{1,0:T(8,128)}, f32[768,3...) conditional(s32[]{:T(128)} %convert_element_type.367, ...), branch_computations={%region_10.31_spmd, %region_31.40_spmd} | conditional | flops 24617672704 | bytes 568646528
  41.1 1.7 slice_reduce_fusion.19
  42.8 1.7 fusion.366
  45.2 1.5 fusion.148
  46.7 2.1 copy.127
  51.2 2.2 fusion.161
  53.4 2.1 fusion.367
  55.5 2.5 convolution_convert_fusion.2
  58.0 1.8 fusion.368
  61.3 9.4 fusion.163
  70.6 4.8 broadcast_in_dim.415
  75.4 4.3 broadcast_in_dim.416
  79.7 3.3 broadcast_in_dim.413
  82.9 1.6 broadcast_in_dim.414
  85.8 89.3 %collective-permute-start.1 = (bf16[128,768]{1,0:T(8,128)(2,1)S(1)}, bf16[128,768]{1,0:T(8,128)(2,1)S(1)}, u32[]{:S(2)}, u32[]{:S(2)}) collective-permute-start(bf16[128,768]{1,0:T(8,128)(2,1)S(1)} %get-tuple-element.681), channel_id=1, source_target_pairs={{0,1},{1,0},{2,3},{3,2},{4,5},{5,4},{6,7},{7,6},{8,9},{9,8},{10,11... | collective-permute-start | bytes 589832 | tf_op jit(solution)/shard_map/ppermute | solution.py:22
  176.7 81.7 %conditional.11 = (bf16[128,768]{1,0:T(8,128)(2,1)S(1)}, f32[768,2304]{1,0:T(8,128)}, f32[768,768]{1,0:T(8,128)}, f32[768,3072]{1,0:T(8,128)}, f32[3072,768]{1,0...) conditional(s32[]{:T(128)} %convert_element_type.367, ...), branch_computations={%region_40.61_spmd, %region_61.84_spmd} | conditional | flops 24624859136 | bytes 583306112
  185.3 1.6 slice_reduce_fusion.36
  187.6 1.7 fusion.376
  190.1 1.5 fusion.289
  191.7 2.1 copy.135
  196.3 1.4 fusion.377
  197.9 1.3 convolution_convert_fusion.6
  200.2 3.7 convolution_add_fusion.20
  203.9 5.5 convert_reduce_fusion.8
  209.4 2.3 multiply_reduce_fusion.22
  215.4 1.8 copy.137
  218.0 1.7 multiply_reduce_fusion.20
  222.1 2.0 multiply_reduce_fusion.21
  224.8 2.7 gather_fusion
  228.3 8.9 convolution_add_fusion.18
  237.4 7.2 convolution_add_fusion.16
  244.6 9.4 convolution_add_fusion.17
  254.0 3.5 convolution_add_fusion.21
  258.4 80.6 %collective-permute-start.2 = (bf16[128,768]{1,0:T(8,128)(2,1)S(1)}, bf16[128,768]{1,0:T(8,128)(2,1)S(1)}, u32[]{:S(2)}, u32[]{:S(2)}) collective-permute-start(bf16[128,768]{1,0:T(8,128)(2,1)S(1)} %get-tuple-element.698), channel_id=1, source_target_pairs={{0,1},{1,0},{2,3},{3,2},{4,5},{5,4},{6,7},{7,6},{8,9},{9,8},{10,11... | collective-permute-start | bytes 589832 | tf_op jit(solution)/shard_map/ppermute | solution.py:22
  340.1 66.0 %conditional.10 = (bf16[512,768]{1,0:T(8,128)(2,1)}, f32[768,2304]{1,0:T(8,128)}, f32[768,768]{1,0:T(8,128)}, f32[768,3072]{1,0:T(8,128)}, f32[3072,768]{1,0:T(8...) conditional(s32[]{:T(128)} %convert_element_type.367, (f32[768,2304]{1,0:T(8,128)}, ...), branch_computations={%region_84.85_spmd, %region_85.108_spmd} | conditional | flops 5159115776 | bytes 217875232 | solution.py:312
  340.1 1.6 slice_reduce_fusion.44
  342.4 1.7 fusion.380
  344.9 2.7 fusion.317
  351.1 3.7 convolution_add_fusion.28
  354.9 5.5 convert_reduce_fusion.12
  360.4 2.3 multiply_reduce_fusion.28
  366.7 1.9 convolution_bitcast_fusion.1
  369.1 2.0 multiply_reduce_fusion.29
  372.4 8.9 convolution_add_fusion.26
  381.4 7.2 convolution_add_fusion.24
  388.7 9.3 convolution_add_fusion.25
  398.1 3.5 convolution_add_fusion.29
  401.7 2.7 gather_fusion.1
  407.1 1.7 copy.168
  412.6 78.5 %all-reduce.2 = f32[3072]{0:T(1024)S(1)} all-reduce(f32[3072]{0:T(1024)} %get-tuple-element.705), channel_id=7, replica_groups=mesh['dp'=16,'pipe'=2] {'dp'}, use_global_device_ids=true, to_apply=%region_113.114.clone | all-reduce | flops 3072 | bytes 24576
  491.8 1.5 select_bitcast_fusion.1
  494.6 36.9 %reduce-scatter.19.cloned.1.call-done = f32[48,2]{1,0:T(8,128)} async-done(((f32[768,2]{1,0:T(8,128)}), f32[48,2]{1,0:T(8,128)}) %reduce-scatter.19.cloned.1.call-update) | async-done | bytes 400
  531.4 1.4 copy.167
  532.8 124.7 %reduce-scatter.21.cloned.1.call-done = f32[48,7]{1,0:T(8,128)} async-done(((f32[768,7]{1,0:T(8,128)}), f32[48,7]{1,0:T(8,128)}) %reduce-scatter.21.cloned.1.call-update) | async-done | bytes 1360
  658.9 130.8 %reduce-scatter.13.cloned.1.call-done = f32[48,768]{1,0:T(8,128)} async-done(((f32[768,768]{1,0:T(8,128)}), f32[48,768]{1,0:T(8,128)}) %reduce-scatter.13.cloned.1.call-update) | async-done | bytes 147472 | tf_op jit(solution)/shard_map/reduce_scatter | solution.py:320
  789.7 155.9 %reduce-scatter.11.cloned.1.call-done = f32[48,2304]{1,0:T(8,128)} async-done(((f32[768,2304]{1,0:T(8,128)}), f32[48,2304]{1,0:T(8,128)}) %reduce-scatter.11.cloned.1.call-update) | async-done | bytes 442384 | tf_op jit(solution)/shard_map/reduce_scatter | solution.py:319
  945.6 176.3 %reduce-scatter.15.cloned.1.call-done = f32[48,3072]{1,0:T(8,128)} async-done(((f32[768,3072]{1,0:T(8,128)}), f32[48,3072]{1,0:T(8,128)}) %reduce-scatter.15.cloned.1.call-update) | async-done | bytes 589840 | tf_op jit(solution)/shard_map/reduce_scatter | solution.py:321
  1121.9 176.1 %reduce-scatter.17.cloned.1.call-done = f32[192,768]{1,0:T(8,128)} async-done(((f32[3072,768]{1,0:T(8,128)}), f32[192,768]{1,0:T(8,128)}) %reduce-scatter.17.cloned.1.call-update) | async-done | bytes 589840 | tf_op jit(solution)/shard_map/reduce_scatter | solution.py:322
  (472 shorter events, 50.2 us)
Async XLA Ops:
  7.2 524.3 %reduce-scatter.19.cloned.1.call-start = ((), (), s32[]{:S(2)}) async-start(), calls=%async_computation.10 | async-start | bytes 417792
  29.5 3.0 collective-permute-start
  33.0 143.6 %copy-start.122 = (f32[1,2,768]{2,1,0:T(2,128)S(1)}, f32[1,2,768]{2,1,0:T(2,128)}, u32[]{:S(2)}) copy-start(f32[1,2,768]{2,1,0:T(2,128)} %param.33) | copy-start | bytes 18436
  85.8 90.9 %copy-start.105 = (bf16[512,768]{1,0:T(8,128)(2,1)}, bf16[512,768]{1,0:T(8,128)(2,1)S(1)}, u32[]{:S(2)}) copy-start(bf16[512,768]{1,0:T(8,128)(2,1)S(1)} %get-tuple-element.690) | copy-start | bytes 2359300
  85.8 90.4 %collective-permute-start.1 = (bf16[128,768]{1,0:T(8,128)(2,1)S(1)}, bf16[128,768]{1,0:T(8,128)(2,1)S(1)}, u32[]{:S(2)}, u32[]{:S(2)}) collective-permute-start(bf16[128,768]{1,0:T(8,128)(2,1)S(1)} %get-tuple-element.681), channel_id=1, source_target_pairs={{0,1},{1,0},{2,3},{3,2},{4,5},{5,4},{6,7},{7,6},{8,9},{9,8},{10,11... | collective-permute-start | bytes 589832 | tf_op jit(solution)/shard_map/ppermute | solution.py:22
  199.4 4.5 copy-start.260
  199.9 11.9 copy-start.35
  199.9 11.9 copy-start.216
  200.1 11.7 copy-start.229
  200.2 3.7 copy-start.89
  200.2 9.3 slice-start.10
  203.9 5.5 copy-start.95
  203.9 5.5 slice-start.11
  228.2 9.0 copy-start.116
  228.2 9.0 copy-start.201
  228.3 9.0 copy-start.197
  228.3 9.0 copy-start.134
  228.3 9.0 copy-start.31
  228.3 9.0 copy-start.58
  228.3 9.0 copy-start.155
  228.3 9.0 copy-start.212
  228.3 9.0 copy-start.225
  237.3 7.2 copy-start.91
  237.3 7.2 copy-start.96
  244.6 9.4 copy-start.85
  244.6 9.4 copy-start.100
  253.9 3.5 copy-start.147
  258.4 81.7 %collective-permute-start.2 = (bf16[128,768]{1,0:T(8,128)(2,1)S(1)}, bf16[128,768]{1,0:T(8,128)(2,1)S(1)}, u32[]{:S(2)}, u32[]{:S(2)}) collective-permute-start(bf16[128,768]{1,0:T(8,128)(2,1)S(1)} %get-tuple-element.698), channel_id=1, source_target_pairs={{0,1},{1,0},{2,3},{3,2},{4,5},{5,4},{6,7},{7,6},{8,9},{9,8},{10,11... | collective-permute-start | bytes 589832 | tf_op jit(solution)/shard_map/ppermute | solution.py:22
  340.1 4.8 copy-start.107
  340.1 7.5 copy-start.135
  341.7 5.9 copy-start.156
  344.1 5.6 copy-start.32
  348.8 17.1 %copy-start.41 = (f32[12,128,128]{1,2,0:T(8,128)}, f32[12,128,128]{1,2,0:T(8,128)S(1)}, u32[]{:S(2)}) copy-start(f32[12,128,128]{1,2,0:T(8,128)S(1)} %get-tuple-element.927) | copy-start | bytes 2359300 | tf_op jit(solution)/shard_map/cond
  349.7 5.1 copy-start.101
  350.4 4.5 copy-start.261
  350.8 11.9 copy-start.37
  350.8 11.9 copy-start.218
  351.0 11.7 copy-start.231
  351.1 3.8 copy-start.108
  351.1 9.3 slice-start.12
  354.8 5.5 copy-start.97
  354.9 5.5 slice-start.13
  372.3 9.0 copy-start.118
  372.4 8.9 copy-start.34
  372.4 8.9 copy-start.60
  372.4 8.9 copy-start.157
  372.4 8.9 copy-start.215
  372.4 8.9 copy-start.228
  381.4 7.3 copy-start.202
  381.4 7.3 copy-start.198
  381.4 7.3 copy-start.136
  381.4 7.3 copy-start.98
  381.4 7.3 copy-start.110
  388.7 9.4 copy-start.137
  388.7 9.4 copy-start.87
  388.7 9.4 copy-start.102
  398.1 3.5 copy-start.130
  401.7 4.0 copy-start.138
  407.0 250.4 %reduce-scatter.21.cloned.1.call-start = ((), (), s32[]{:S(2)}) async-start(), calls=%async_computation.11 | async-start | bytes 417792
  408.8 380.9 %reduce-scatter.13.cloned.1.call-start = ((), (), s32[]{:S(2)}) async-start(), calls=%async_computation.7 | async-start | bytes 2506752 | tf_op jit(solution)/shard_map/reduce_scatter | solution.py:320
  409.5 536.1 %reduce-scatter.11.cloned.1.call-start = ((), (), s32[]{:S(2)}) async-start(), calls=%async_computation.6 | async-start | bytes 7520256 | tf_op jit(solution)/shard_map/reduce_scatter | solution.py:319
  410.1 711.8 %reduce-scatter.15.cloned.1.call-start = ((), (), s32[]{:S(2)}) async-start(), calls=%async_computation.8 | async-start | bytes 10027008 | tf_op jit(solution)/shard_map/reduce_scatter | solution.py:321
  410.7 887.4 %reduce-scatter.17.cloned.1.call-start = ((), (), s32[]{:S(2)}) async-start(), calls=%async_computation.9 | async-start | bytes 10027008 | tf_op jit(solution)/shard_map/reduce_scatter | solution.py:322
  410.7 81.0 %copy-start.106 = (bf16[512,768]{1,0:T(8,128)(2,1)S(1)}, bf16[512,768]{1,0:T(8,128)(2,1)}, u32[]{:S(2)}) copy-start(bf16[512,768]{1,0:T(8,128)(2,1)} %copy-done.105) | copy-start | bytes 2359300
  (94 other events, 173.7 us)
Sparse Core Ops, SparseCore 0:
  407.1 124.2 reduce-scatter.18
  536.8 120.6 reduce-scatter.20
  662.9 126.6 reduce-scatter.12
  796.3 149.2 reduce-scatter.10
  952.7 169.1 reduce-scatter.14
  1128.0 169.9 reduce-scatter.16
where the time goes:
time: 1320 us; the launch traced here: 1310 us
  waiting for transfers between devices  805 us (61%)
  starting transfers between devices  170 us (13%)
  matrix products  141 us (11%)
  blocking collectives  78.5 us (6%)
  local copies, waits for them, and re-layouts  55.5 us (4%)
  other arithmetic  21.2 us (2%)
  loops' own time  18.3 us (1%)
  between operations  15.5 us (1%)
    reduce_scatter x1, waiting for transfers between devices, on_device(): lax.psum_scatter(grad_sums[2], 'dp', scatter_dimension=0, tiled=True)  176 us
    reduce_scatter x1, waiting for transfers between devices, on_device(): lax.psum_scatter(grad_sums[3], 'dp', scatter_dimension=0, tiled=True)  176 us
    ppermute x3, starting transfers between devices, swapped(): return lax.ppermute(value, axis, pairs)  170 us
    unnamed x8, waiting for transfers between devices  164 us
    reduce_scatter x1, waiting for transfers between devices, on_device(): lax.psum_scatter(grad_sums[0], 'dp', scatter_dimension=0, tiled=True)  156 us
    reduce_scatter x1, waiting for transfers between devices, on_device(): lax.psum_scatter(grad_sums[1], 'dp', scatter_dimension=0, tiled=True)  131 us
    unnamed x1, blocking collectives  78.5 us
  transfers between devices with their start and end apart: 9, of which 8 were waited for; matrix products, arithmetic and copies ran while one was open for 1% of the time, Pallas kernels for 0%

commit v1 on v0

v1 whole, which is shorter than its diff:
```python
import functools
import math

import jax
import jax.numpy as jnp
import numpy as np
from jax import lax
from jax.experimental import pallas as pl
from jax.experimental.pallas import tpu as pltpu
from jax.sharding import PartitionSpec as P

D = 768
H = 12
HD = 64
FF = 3072
S = 512
VIS = 128
MICRO = 2
EPSILON = 1e-06
PAIRS = H // 2
TWO = 2 * HD
TILES = FF // D
HALF = D // 2
GROUPS = 16
GROUP_ROWS = D // GROUPS
ROWS = 16
F32 = jnp.float32
BF16 = jnp.bfloat16

SHIFT1, QBIAS, VBIAS, OBIAS, ENTRY, SHIFT2, DBIAS, GAIN1, GAIN2, UBIAS = range(10)


def contract(left, right, left_dim, right_dim):
    return lax.dot_general(
        left, right, (((left_dim,), (right_dim,)), ((), ())), preferred_element_type=F32
    )


def nn(left, right):
    return contract(left, right, 1, 0)


def nt(left, right):
    return contract(left, right, 1, 1)


def unit_rows(rows):
    centered = rows - jnp.mean(rows, axis=-1, keepdims=True)
    scale = lax.rsqrt(jnp.mean(centered * centered, axis=-1, keepdims=True) + EPSILON)
    return centered * scale, scale


def unit_rows_back(grad, unit, scale, gain):
    scaled = grad * gain
    return scale * (
        scaled
        - jnp.mean(scaled, axis=-1, keepdims=True)
        - unit * jnp.mean(scaled * unit, axis=-1, keepdims=True)
    )


def one_head(pair, which):
    lane = lax.broadcasted_iota(jnp.int32, pair.shape, 1)
    inside = lane < HD if which == 0 else lane >= HD
    return jnp.where(inside, pair, jnp.zeros_like(pair))


def hits(slots, dim):
    shape = (S, VIS) if dim == 0 else (VIS, S)
    return lax.broadcasted_iota(jnp.int32, shape, 1 - dim) == slots


def colsum(rows):
    return jnp.sum(rows, axis=0, keepdims=True)


def row(ref, index):
    return ref[index : index + 1, :]


class Pair:
    def __init__(self, refs):
        self.refs = refs

    def get(self, core):
        if len(self.refs) == 1:
            return self.refs[0][...]
        return jnp.where(core == 0, self.refs[1][...], self.refs[0][...])


def either(arrays, shape, index):
    if len(arrays) == 1:
        return [pl.BlockSpec(shape, lambda i, core: index(i))]
    zero = (0,) * len(shape)

    def on(wanted):
        def place(i, core):
            return tuple(
                jnp.where(core[0] == wanted, at, z) for at, z in zip(index(i), zero)
            )

        return place

    return [pl.BlockSpec(shape, on(1)), pl.BlockSpec(shape, on(0))]


def whole(shape):
    return pl.BlockSpec(shape, lambda i, core: (0,) * len(shape))


def struct(shape, dtype):
    return jax.ShapeDtypeStruct(shape, dtype)


def call(body, core, grid, ins, outs, scratch, name, flops):
    in_specs, args = [], []
    for specs, arrays in ins:
        in_specs += specs
        args += arrays
    out_specs = [spec for spec, _ in outs]
    out_shape = [shape for _, shape in outs]
    moved = sum(math.prod(a.shape) * a.dtype.itemsize for a in args)
    moved += sum(math.prod(a.shape) * a.dtype.itemsize for a in out_shape)
    return pl.pallas_call(
        body,
        grid_spec=pltpu.PrefetchScalarGridSpec(
            num_scalar_prefetch=1,
            grid=(grid,),
            in_specs=in_specs,
            out_specs=out_specs,
            scratch_shapes=scratch,
        ),
        out_shape=out_shape,
        compiler_params=pltpu.CompilerParams(
            vmem_limit_bytes=56 * 2**20, dimension_semantics=("arbitrary",)
        ),
        cost_estimate=pl.CostEstimate(flops=flops, bytes_accessed=moved, transcendentals=0),
        name=name,
    )(core, *args)


def attention_forward_body(n, decoder, core_ref, *refs):
    core = core_ref[0]
    refs = list(refs)
    take = lambda count: [refs.pop(0) for _ in range(count)]
    params_ref, slot_col, slot_row, img_col, img_row = take(5)
    sources = take(2 if decoder else 1)
    many = 2 if decoder else 1
    wq, wk, wv = Pair(take(many)), Pair(take(many)), Pair(take(many))
    x_ref, h_ref, qkv_ref, att_ref, lse_ref, bias_ref = refs
    j = pl.program_id(0)

    @pl.when(j == 0)
    def _():
        if decoder:
            sent_ref, pos_ref = sources
            slots = slot_col[0]
            hit = hits(slots, 0).astype(BF16)
            x = nn(hit, sent_ref[...]) + pos_ref[...]
            x = x + jnp.where(slots == VIS, row(params_ref, ENTRY), 0.0)
            x_ref[...] = x
            bias_ref[...] = jnp.where(img_col[0] == img_row[0], 0.0, -1e30)
        else:
            (patches_ref,) = sources
            cols, rows = [], []
            for micro in range(MICRO):
                hit = hits(slot_row[micro], 1)
                x_ref[micro * VIS : (micro + 1) * VIS, :] = nn(
                    hit.astype(BF16), patches_ref[micro]
                ) + row(params_ref, ENTRY)
                mark = img_row[micro] + 1
                cols.append(
                    jnp.sum(jnp.where(hit, mark, 0).astype(F32), axis=1, keepdims=True)
                    + 4.0 * micro
                )
                mark = img_col[micro] + 1
                rows.append(
                    jnp.sum(
                        jnp.where(hits(slot_col[micro], 0), mark, 0).astype(F32),
                        axis=0,
                        keepdims=True,
                    )
                    + 4.0 * micro
                )
            bias_ref[...] = jnp.where(
                jnp.concatenate(cols, axis=0) == jnp.concatenate(rows, axis=1), 0.0, -1e30
            )
        unit, _scale = unit_rows(x_ref[...])
        h_ref[...] = (unit * row(params_ref, GAIN1) + row(params_ref, SHIFT1)).astype(BF16)

    lanes = pl.ds(pl.multiple_of(j * TWO, TWO), TWO)
    h = h_ref[...]
    q = (nn(h, wq.get(core)) + params_ref[QBIAS : QBIAS + 1, lanes]).astype(BF16)
    k = nn(h, wk.get(core)).astype(BF16)
    v_wide = nn(h, wv.get(core)) + params_ref[VBIAS : VBIAS + 1, lanes]
    v = v_wide.astype(BF16)
    qkv_ref[0] = q
    qkv_ref[1] = k
    qkv_ref[2] = v
    v_across = v_wide.T.astype(BF16)
    bias = bias_ref[...]
    found = []
    for which in range(2):
        scaled = one_head(q, which) * jnp.asarray(HD**-0.5, BF16)
        scores = nt(k, scaled) + bias
        top = jnp.max(scores, axis=0, keepdims=True)
        raised = jnp.exp(scores - top)
        total = jnp.sum(raised, axis=0, keepdims=True)
        part = nn(v_across[which * HD : (which + 1) * HD, :], raised.astype(BF16))
        found.append(part * (1.0 / total))
        lse_ref[0, which : which + 1, :] = top + jnp.log(total)
    att_ref[...] = jnp.concatenate(found, axis=0).T.astype(BF16)


def attention_forward(core, n, decoder, params, marks, sources, w_qkv):
    slot_col, slot_row, img_col, img_row = marks
    m = slot_col.shape[0]
    ins = [
        ([whole((ROWS, D))], [params]),
        ([whole((m, S, 1))], [slot_col]),
        ([whole((m, 1, S))], [slot_row]),
        ([whole((m, S, 1))], [img_col]),
        ([whole((m, 1, S))], [img_row]),
    ]
    ins += [([whole(source.shape)], [source]) for source in sources]
    for part in range(3):
        ins.append(
            (either(w_qkv, (D, TWO), lambda j, part=part: (0, part * PAIRS + j)), list(w_qkv))
        )
    outs = [
        (whole((n, D)), struct((n, D), F32)),
        (whole((n, D)), struct((n, D), BF16)),
        (pl.BlockSpec((3, n, TWO), lambda j, core: (0, 0, j)), struct((3, n, D), BF16)),
        (pl.BlockSpec((n, TWO), lambda j, core: (0, j)), struct((n, D), BF16)),
        (pl.BlockSpec((1, 8, n), lambda j, core: (j, 0, 0)), struct((PAIRS, 8, n), F32)),
        (whole((n, n)), struct((n, n), F32)),
    ]
    return call(
        functools.partial(attention_forward_body, n, decoder),
        core,
        PAIRS,
        ins,
        outs,
        [],
        "attention_forward",
        2 * n * D * 3 * D + 4 * n * n * D,
    )


def feed_forward_body(many, core_ref, *refs):
    core = core_ref[0]
    refs = list(refs)
    take = lambda count: [refs.pop(0) for _ in range(count)]
    params_ref, x_ref, att_ref = take(3)
    w_out, w_up, w_down = Pair(take(many)), Pair(take(many)), Pair(take(many))
    mid_ref, h2_ref, act_ref, slope_ref, out_ref, sum_ref = refs
    t = pl.program_id(0)

    @pl.when(t == 0)
    def _():
        mid = x_ref[...] + nn(att_ref[...], w_out.get(core)) + row(params_ref, OBIAS)
        mid_ref[...] = mid
        unit, _scale = unit_rows(mid)
        h2_ref[...] = (unit * row(params_ref, GAIN2) + row(params_ref, SHIFT2)).astype(BF16)
        sum_ref[...] = mid + row(params_ref, DBIAS)

    pre = nn(h2_ref[...], w_up.get(core)) + params_ref[pl.ds(UBIAS + t, 1), :]
    below = 0.5 + 0.5 * lax.erf(pre * math.sqrt(0.5))
    act = (pre * below).astype(BF16)
    act_ref[...] = act
    density = jnp.exp(-0.5 * pre * pre) * (1.0 / math.sqrt(2.0 * math.pi))
    slope_ref[...] = (below + pre * density).astype(BF16)
    sum_ref[...] += nn(act, w_down.get(core))

    @pl.when(t == TILES - 1)
    def _():
        out_ref[...] = sum_ref[...].astype(BF16)


def feed_forward(core, n, params, x, att, w_out, w_up, w_down):
    ins = [
        ([whole((ROWS, D))], [params]),
        ([whole((n, D))], [x]),
        ([whole((n, D))], [att]),
        (either(w_out, (D, D), lambda t: (0, 0)), list(w_out)),
        (either(w_up, (D, D), lambda t: (0, t)), list(w_up)),
        (either(w_down, (D, D), lambda t: (t, 0)), list(w_down)),
    ]
    tile = pl.BlockSpec((n, D), lambda t, core: (0, t))
    outs = [
        (whole((n, D)), struct((n, D), F32)),
        (whole((n, D)), struct((n, D), BF16)),
        (tile, struct((n, FF), BF16)),
        (tile, struct((n, FF), BF16)),
        (whole((n, D)), struct((n, D), BF16)),
    ]
    return call(
        functools.partial(feed_forward_body, len(w_out)),
        core,
        TILES,
        ins,
        outs,
        [pltpu.VMEM((n, D), F32)],
        "feed_forward",
        2 * n * (D * D + 2 * D * FF),
    )


def halves(core, value):
    left, right = value[:, :HALF].astype(BF16), value[:, HALF:].astype(BF16)
    return jnp.where(core == 0, left, right), jnp.where(core == 0, right, left)


def feed_backward_body(many, core_ref, *refs):
    core = core_ref[0]
    refs = list(refs)
    take = lambda count: [refs.pop(0) for _ in range(count)]
    params_ref = take(1)[0]
    dy = Pair(take(many))
    act_ref, slope_ref, h2_ref, mid_ref, att_ref = take(5)
    w_out, w_up, w_down = Pair(take(many)), Pair(take(many)), Pair(take(many))
    up_keep, up_send, down_keep, down_send, dmid_ref, datt_ref, small_ref = take(7)
    dff_ref, h2_across, dh2_ref = refs
    t = pl.program_id(0)

    @pl.when(t == 0)
    def _():
        dff = dy.get(core)
        dff_ref[...] = dff
        h2_across[...] = h2_ref[...].T
        dh2_ref[...] = jnp.zeros_like(dh2_ref)
        small_ref[...] = jnp.zeros_like(small_ref)
        small_ref[DBIAS : DBIAS + 1, :] = colsum(dff.astype(F32))

    @pl.when(t < TILES)
    def _():
        dff = dff_ref[...]
        keep, send = halves(core, nn(act_ref[...].T, dff))
        per = D // down_keep.shape[0]
        down_keep[...] = keep.reshape(down_keep.shape)
        down_send[...] = send.reshape(down_send.shape)
        dpre_wide = nt(dff, w_down.get(core)) * slope_ref[...].astype(F32)
        dpre = dpre_wide.astype(BF16)
        small_ref[pl.ds(UBIAS + t, 1), :] = colsum(dpre.astype(F32))
        keep, send = halves(core, nn(h2_across[...], dpre))
        up_keep[...] = keep.reshape(up_keep.shape)
        up_send[...] = send.reshape(up_send.shape)
        dh2_ref[...] += nt(dpre, w_up.get(core))

    @pl.when(t == TILES)
    def _():
        dh2 = dh2_ref[...]
        unit, scale = unit_rows(mid_ref[...])
        small_ref[GAIN2 : GAIN2 + 1, :] = colsum(dh2 * unit)
        small_ref[SHIFT2 : SHIFT2 + 1, :] = colsum(dh2)
        dmid = dff_ref[...].astype(F32) + unit_rows_back(
            dh2, unit, scale, row(params_ref, GAIN2)
        )
        dmid_ref[...] = dmid
        dbranch = dmid.astype(BF16)
        small_ref[OBIAS : OBIAS + 1, :] = colsum(dbranch.astype(F32))
        keep, send = halves(core, nn(att_ref[...].T, dbranch))
        up_keep[...] = keep.reshape(up_keep.shape)
        up_send[...] = send.reshape(up_send.shape)
        datt_ref[...] = nt(dbranch, w_out.get(core)).astype(BF16)


def feed_backward(core, n, params, dy, act, slope, h2, mid, att, w_out, w_up, w_down):
    last = TILES - 1
    tile = pl.BlockSpec((n, D), lambda t, core: (0, jnp.minimum(t, last)))
    ins = [
        ([whole((ROWS, D))], [params]),
        (either(dy, (n, D), lambda t: (0, 0)), list(dy)),
        ([tile], [act]),
        ([tile], [slope]),
        ([whole((n, D))], [h2]),
        ([whole((n, D))], [mid]),
        ([whole((n, D))], [att]),
        (either(w_out, (D, D), lambda t: (0, 0)), list(w_out)),
        (either(w_up, (D, D), lambda t: (0, jnp.minimum(t, last))), list(w_up)),
        (either(w_down, (D, D), lambda t: (jnp.minimum(t, last), 0)), list(w_down)),
    ]
    up_spec = pl.BlockSpec((GROUPS, 1, GROUP_ROWS, HALF), lambda t, core: (0, t, 0, 0))
    up_shape = struct((GROUPS, TILES + 1, GROUP_ROWS, HALF), BF16)
    per = GROUPS // TILES
    down_spec = pl.BlockSpec(
        (per, D // per, HALF), lambda t, core: (jnp.minimum(t, last), 0, 0)
    )
    down_shape = struct((GROUPS, D // per, HALF), BF16)
    outs = [
        (up_spec, up_shape),
        (up_spec, up_shape),
        (down_spec, down_shape),
        (down_spec, down_shape),
        (whole((n, D)), struct((n, D), F32)),
        (whole((n, D)), struct((n, D), BF16)),
        (whole((ROWS, D)), struct((ROWS, D), F32)),
    ]
    return call(
        functools.partial(feed_backward_body, len(w_out)),
        core,
        TILES + 1,
        ins,
        outs,
        [pltpu.VMEM((n, D), BF16), pltpu.VMEM((D, n), BF16), pltpu.VMEM((n, D), F32)],
        "feed_backward",
        4 * n * (D * D + 2 * D * FF),
    )


def attention_backward_body(n, decoder, core_ref, *refs):
    core = core_ref[0]
    refs = list(refs)
    take = lambda count: [refs.pop(0) for _ in range(count)]
    many = 2 if decoder else 1
    params_ref, x_ref, h_ref, qkv_ref, att_ref, datt_ref, lse_ref, bias_ref = take(8)
    wq, wk, wv = Pair(take(many)), Pair(take(many)), Pair(take(many))
    dmid_ref, small_in, slot_col, slot_row = take(4)
    keep_ref, send_ref, small_ref, back_ref = take(4)
    h_across, dh_ref = refs
    j = pl.program_id(0)

    @pl.when(j == 0)
    def _():
        h_across[...] = h_ref[...].T
        dh_ref[...] = jnp.zeros_like(dh_ref)
        small_ref[...] = small_in[...]

    q, k, v = qkv_ref[0], qkv_ref[1], qkv_ref[2]
    datt = datt_ref[...]
    bias = bias_ref[...]
    along = (att_ref[...].astype(F32) * datt.astype(F32)).T
    k_across = k.T
    dq, dk, dv = [], 0.0, 0.0
    for which in range(2):
        scaled = one_head(q, which) * jnp.asarray(HD**-0.5, BF16)
        mine = one_head(datt, which)
        probs = jnp.exp(nt(k, scaled) + bias - lse_ref[0, which : which + 1, :])
        delta = colsum(along[which * HD : (which + 1) * HD, :])
        dscores = (probs * (nt(v, mine) - delta)).astype(BF16)
        dv = dv + nn(probs.astype(BF16), mine)
        dk = dk + nn(dscores, scaled)
        dq.append(nn(k_across[which * HD : (which + 1) * HD, :], dscores))
    dq = (jnp.concatenate(dq, axis=0) * HD**-0.5).T.astype(BF16)
    dk = dk.astype(BF16)
    dv = dv.astype(BF16)
    at = lax.rem(j + PAIRS // 2 * (1 - core), PAIRS)
    lanes = pl.ds(pl.multiple_of(at * TWO, TWO), TWO)
    small_ref[QBIAS : QBIAS + 1, lanes] = colsum(dq.astype(F32))
    small_ref[VBIAS : VBIAS + 1, lanes] = colsum(dv.astype(F32))
    across = h_across[...]
    grads = [nn(across, part).astype(BF16) for part in (dq, dk, dv)]

    @pl.when(j < PAIRS // 2)
    def _():
        for part in range(3):
            send_ref[:, part] = grads[part].reshape(GROUPS, GROUP_ROWS, TWO)

    @pl.when(j >= PAIRS // 2)
    def _():
        for part in range(3):
            keep_ref[:, part] = grads[part].reshape(GROUPS, GROUP_ROWS, TWO)

    dh_ref[...] += nt(dq, wq.get(core)) + nt(dk, wk.get(core)) + nt(dv, wv.get(core))

    @pl.when(j == PAIRS - 1)
    def _():
        dh = dh_ref[...]
        unit, scale = unit_rows(x_ref[...])
        small_ref[GAIN1 : GAIN1 + 1, :] = colsum(dh * unit)
        small_ref[SHIFT1 : SHIFT1 + 1, :] = colsum(dh)
        dx = dmid_ref[...] + unit_rows_back(dh, unit, scale, row(params_ref, GAIN1))
        low = dx.astype(BF16)
        if decoder:
            small_ref[ENTRY : ENTRY + 1, :] = colsum(jnp.where(slot_col[0] == VIS, dx, 0.0))
            back_ref[...] = nn(hits(slot_row[0], 1).astype(BF16), low).astype(BF16)
        else:
            small_ref[ENTRY : ENTRY + 1, :] = colsum(dx)
            for micro in range(MICRO):
                back_ref[micro] = nn(
                    hits(slot_col[micro], 0).astype(BF16),
                    low[micro * VIS : (micro + 1) * VIS, :],
                ).astype(BF16)


def attention_backward(
    core, n, decoder, params, x, h, qkv, att, datt, lse, bias, w_qkv, dmid, small, marks
):
    slot_col, slot_row = marks[:2]
    m = slot_col.shape[0]
    mid = PAIRS // 2

    def turn(j, core):
        return lax.rem(j + mid * (1 - core[0]), PAIRS)

    ins = [
        ([whole((ROWS, D))], [params]),
        ([whole((n, D))], [x]),
        ([whole((n, D))], [h]),
        ([pl.BlockSpec((3, n, TWO), lambda j, core: (0, 0, turn(j, core)))], [qkv]),
        ([pl.BlockSpec((n, TWO), lambda j, core: (0, turn(j, core)))], [att]),
        ([pl.BlockSpec((n, TWO), lambda j, core: (0, turn(j, core)))], [datt]),
        ([pl.BlockSpec((1, 8, n), lambda j, core: (turn(j, core), 0, 0))], [lse]),
        ([whole((n, n))], [bias]),
    ]
    for part in range(3):
        specs = []
        for wanted in (None,) if len(w_qkv) == 1 else (1, 0):

            def place(j, core, part=part, wanted=wanted):
                at = part * PAIRS + turn(j, core)
                return (0, at if wanted is None else jnp.where(core[0] == wanted, at, 0))

            specs.append(pl.BlockSpec((D, TWO), place))
        ins.append((specs, list(w_qkv)))
    ins += [
        ([whole((n, D))], [dmid]),
        ([whole((ROWS, D))], [small]),
        ([whole((m, S, 1))], [slot_col]),
        ([whole((m, 1, S))], [slot_row]),
    ]
    block = (GROUPS, 3, GROUP_ROWS, TWO)
    shape = struct((GROUPS, 3, GROUP_ROWS, HALF), BF16)
    back = (VIS, D) if decoder else (MICRO, S, D)
    outs = [
        (pl.BlockSpec(block, lambda j, core: (0, 0, 0, jnp.maximum(j - mid, 0))), shape),
        (pl.BlockSpec(block, lambda j, core: (0, 0, 0, jnp.minimum(j, mid - 1))), shape),
        (whole((ROWS, D)), struct((ROWS, D), F32)),
        (whole(back), struct(back, BF16)),
    ]
    return call(
        functools.partial(attention_backward_body, n, decoder),
        core,
        PAIRS,
        ins,
        outs,
        [pltpu.VMEM((D, n), BF16), pltpu.VMEM((n, D), F32)],
        "attention_backward",
        4 * n * D * 3 * D + 10 * n * n * D,
    )


def over_pipe(value, pairs):
    return lax.ppermute(value, "pipe", pairs)


SWAP = [(0, 1), (1, 0)]


def add(left, right, dtype):
    return (left.astype(F32) + right.astype(F32)).astype(dtype)


def exchange(piece, bits, bit, dtype=BF16):
    at = bits.index(bit)
    size = lax.axis_size("dp")
    mine = lax.rem(lax.axis_index("dp") // 2**bit, 2)
    send = lax.dynamic_index_in_dim(piece, 1 - mine, at, keepdims=False)
    keep = lax.dynamic_index_in_dim(piece, mine, at, keepdims=False)
    got = lax.ppermute(send, "dp", [(i, i ^ 2**bit) for i in range(size)])
    return add(keep, got, dtype), bits[:at] + bits[at + 1 :]


def by_device(piece):
    size = lax.axis_size("dp")
    more = size // GROUPS
    groups, slabs, rows, columns = piece.shape
    if more > 1:
        piece = piece.reshape(groups, slabs, more, rows // more, columns).transpose(0, 2, 1, 3, 4)
    count = size.bit_length() - 1
    return piece.reshape((2,) * count + (slabs * rows // more, columns)), list(
        range(count - 1, -1, -1)
    )


def scatter_sum(keep, send, first):
    piece = add(keep, over_pipe(send, SWAP), BF16)
    slabs = piece.shape[1]
    piece, bits = by_device(piece)
    order = first + [bit for bit in range(len(bits)) if bit not in first]
    for bit in order:
        piece, bits = exchange(piece, bits, bit, BF16 if len(bits) > 1 else F32)
    return piece.reshape(slabs, -1, HALF)


def everywhere(value):
    value = value + over_pipe(value, SWAP)
    size = lax.axis_size("dp")
    step = 1
    while step < size:
        value = value + lax.ppermute(value, "dp", [(i, i ^ step) for i in range(size)])
        step *= 2
    return value


def positions():
    width = D // 2
    frequency = np.exp(np.arange(width) * (-math.log(10000.0) / width))
    angles = np.arange(S)[:, None] * frequency[None, :]
    return jnp.asarray(np.concatenate([np.sin(angles), np.cos(angles)], axis=1), F32)


def on_device(
    section_input,
    visible_slot,
    image_of_slot,
    qkv_weight,
    out_weight,
    up_weight,
    down_weight,
    norm_gain,
    up_bias,
    vectors,
):
    pipe = lax.axis_index("pipe")
    first = pipe == 0
    core = pipe.astype(jnp.int32)[None]
    own = [qkv_weight[0], out_weight[0], up_weight[0], down_weight[0]]
    params = jnp.concatenate(
        [vectors[0], norm_gain[0], up_bias[0].reshape(TILES, D), jnp.zeros((3, D), F32)]
    )
    to_first, to_second = [(1, 0)], [(0, 1)]
    both = [[weight, over_pipe(weight, to_first)] for weight in own]
    dec_params = jnp.where(first, over_pipe(params, to_first), params)
    cotangent = [section_input[0, 1], over_pipe(section_input[0, 0], to_first)]

    def marks_of(slots, images):
        return (slots[:, :, None], slots[:, None, :], images[:, :, None], images[:, None, :])

    enc_marks = marks_of(visible_slot, image_of_slot)
    dec_marks = marks_of(
        lax.dynamic_index_in_dim(visible_slot, pipe, 0),
        lax.dynamic_index_in_dim(image_of_slot, pipe, 0),
    )
    rows = MICRO * VIS

    x, h, qkv, att, lse, bias = attention_forward(
        core, rows, False, params, enc_marks, [section_input[0]], [own[0]]
    )
    mid, h2, act, slope, out = feed_forward(core, rows, params, x, att, *[[w] for w in own[1:]])
    encoder = (x, h, qkv, att, lse, bias, mid, h2, act, slope)
    sent = jnp.where(first, out[:VIS], over_pipe(out[VIS:], to_second))

    def back(rows, decoder, params, dy, kept, weights, marks):
        x, h, qkv, att, lse, bias, mid, h2, act, slope = kept
        up_keep, up_send, down_keep, down_send, dmid, datt, small = feed_backward(
            core, rows, params, dy, act, slope, h2, mid, att, *weights[1:]
        )
        per = GROUPS // TILES
        down_shape = (GROUPS, 1, D // per, HALF)
        ups = scatter_sum(up_keep, up_send, [0, 1])
        downs = scatter_sum(down_keep.reshape(down_shape), down_send.reshape(down_shape), [1, 0])
        keep, send, small, returned = attention_backward(
            core, rows, decoder, params, x, h, qkv, att, datt, lse, bias, weights[0],
            dmid, small, marks,
        )
        heads = scatter_sum(keep, send, [0, 1])
        return returned, small, (ups, downs, heads)

    x, h, qkv, att, lse, bias = attention_forward(
        core, S, True, dec_params, dec_marks, [sent, positions()], both[0]
    )
    mid, h2, act, slope, out = feed_forward(core, S, dec_params, x, att, *both[1:])
    decoded = jnp.stack([over_pipe(out, to_second), out])
    kept = (x, h, qkv, att, lse, bias, mid, h2, act, slope)
    returned, dec_small, dec_grads = back(S, True, dec_params, cotangent, kept, both, dec_marks)

    other = over_pipe(returned, to_first)
    dy = jnp.where(first, jnp.concatenate([returned, other]), 0)
    returned, enc_small, enc_grads = back(
        rows, False, params, [dy], encoder, [[w] for w in own], enc_marks
    )
    results = jnp.where(first, returned, decoded)

    small = everywhere(jnp.stack([dec_small, enc_small]))
    small = jnp.where(first, small[1], small[0])
    joined = []
    for dec, enc in zip(dec_grads, enc_grads):
        got = over_pipe(jnp.where(first, dec, enc), SWAP)
        joined.append(
            jnp.concatenate(
                [jnp.where(first, enc, got), jnp.where(first, got, dec)], axis=-1
            )
        )
    ups, downs, heads = joined
    place = lax.axis_index("dp")
    width = D // lax.axis_size("dp")
    mine = lax.dynamic_slice_in_dim(small, place * width, width, 1)
    hidden = FF // lax.axis_size("dp")
    bias_grad = lax.dynamic_slice_in_dim(
        small[UBIAS : UBIAS + TILES].reshape(FF), place * hidden, hidden, 0
    )

    def wide(slabs):
        return slabs.transpose(1, 0, 2).reshape(slabs.shape[1], -1)

    return (
        results[None],
        wide(heads)[None],
        ups[TILES][None],
        wide(ups[:TILES])[None],
        downs.reshape(-1, D)[None],
        mine[GAIN1 : GAIN2 + 1][None],
        bias_grad[None],
        mine[:GAIN1][None],
    )


def solution(mesh):
    in_specs = (
        P("pipe", "dp", None, None),
        P("dp", None),
        P("dp", None),
        P("pipe", None, None),
        P("pipe", None, None),
        P("pipe", None, None),
        P("pipe", None, None),
        P("pipe", None, None),
        P("pipe", None),
        P("pipe", None, None),
    )
    out_specs = (
        P("pipe", "dp", None, None),
        P("pipe", "dp", None),
        P("pipe", "dp", None),
        P("pipe", "dp", None),
        P("pipe", "dp", None),
        P("pipe", None, "dp"),
        P("pipe", "dp"),
        P("pipe", None, "dp"),
    )
    return jax.shard_map(
        on_device, mesh=mesh, in_specs=in_specs, out_specs=out_specs, check_vma=False
    )
```

time: 1320 us -> 432 us (0.33)
  waiting for transfers between devices: 805 us -> 154 us
  matrix products: 141 us -> 0 us
  Pallas kernels: 0 us -> 141 us
  starting transfers between devices: 170 us -> 64.3 us
  blocking collectives: 78.5 us -> 0 us
  local copies, waits for them, and re-layouts: 55.5 us -> 32.3 us
  loops' own time: 18.3 us -> 0 us
  between operations: 15.5 us -> 1.61 us
    reduce_scatter x4 -> x0, waiting for transfers between devices: 639 us -> none  [the longest x1 176 us: on_device(): lax.psum_scatter(grad_sums[2], 'dp', scatter_dimension=0, tiled=True)]
    unnamed x8 -> x0, waiting for transfers between devices: 164 us -> none
    ppermute x3 -> x47, waiting for transfers between devices: 2.14 us -> 154 us  [the longest x24 141 us: exchange(): got = lax.ppermute(send, 'dp', [(i, i ^ 2 ** bit) for i in range(size)])]
    pallas_call x0 -> x8, Pallas kernels: none -> 141 us  [call(): pl.pallas_call(body, grid_spec=pltpu.PrefetchScalarGridSpec(num_scalar_pr...]
    dot_general x48 -> x0, matrix products: 139 us -> none  [the longest x2 18.7 us: block_backward(): jnp.einsum('nf,nd->fd', activated, grad_feed, preferred_element_type=jnp....]
    ppermute x3 -> x47, starting transfers between devices: 170 us -> 64.3 us  [the longest x24 31.4 us: exchange(): got = lax.ppermute(send, 'dp', [(i, i ^ 2 ** bit) for i in range(size)])]
    unnamed x1 -> x0, blocking collectives: 78.5 us -> none
    convert_element_type x2 -> x24, other arithmetic: 0.34 us -> 17.3 us  [add(): return (left.astype(F32) + right.astype(F32)).astype(dtype)]
  transfers between devices with their start and end apart: 9 -> 47, of which waited for: 8 -> 21; matrix products, arithmetic and copies ran while one was open for 1% -> 13% of each run, Pallas kernels for 0% -> 12%
where the time goes in v1:
time: 432 us; the launch traced here: 427 us
  waiting for transfers between devices  154 us (36%)
  Pallas kernels  141 us (33%)
  starting transfers between devices  64.3 us (15%)
  other arithmetic  33.2 us (8%)
  local copies, waits for them, and re-layouts  32.3 us (7%)
    pallas_call x8, Pallas kernels, call(): pl.pallas_call(body, grid_spec=pltpu.PrefetchScalarGridSpec(num_scalar_pr...  141 us
    ppermute x24, waiting for transfers between devices, exchange(): got = lax.ppermute(send, 'dp', [(i, i ^ 2 ** bit) for i in range(size)])  141 us
    ppermute x24, starting transfers between devices, exchange(): got = lax.ppermute(send, 'dp', [(i, i ^ 2 ** bit) for i in range(size)])  31.4 us
    ppermute x19, starting transfers between devices, over_pipe(): return lax.ppermute(value, 'pipe', pairs)  22.8 us
    convert_element_type x24, other arithmetic, add(): return (left.astype(F32) + right.astype(F32)).astype(dtype)  17.3 us
    ppermute x4, starting transfers between devices, everywhere(): lax.ppermute(value, 'dp', [(i, i ^ step) for i in range(size)])  10.1 us
    ppermute x4, waiting for transfers between devices, everywhere(): lax.ppermute(value, 'dp', [(i, i ^ step) for i in range(size)])  9.35 us
  transfers between devices with their start and end apart: 47, of which 21 were waited for; matrix products, arithmetic and copies ran while one was open for 13% of the time, Pallas kernels for 12%

profile of v1, /device:TPU:0, one launch (start us, length us, event | category | flops | bytes accessed | tf_op | source)
XLA Modules:
  0.0 426.6 jit_solution(14884560158002133049)
XLA Ops:
  5.0 2.0 reduce.3
  9.1 1.4 maximum_maximum_fusion.refs_0_
  14.3 1.7 copy.41.refs_1_.refs_13_
  17.3 1.7 copy.42.refs_3_
  19.0 9.3 %attention_forward.2 = (f32[256,768]{1,0:T(8,128)}, bf16[256,768]{1,0:T(8,128)(2,1)}, bf16[3,256,768]{2,1,0:T(8,128)(2,1)}, bf16[256,768]{1,0:T(8,128)(2,1)}, f32[6,8,256]{2,1,0:T(8,128)}, /*index=5*/f32[256,256]{1,0:T(8,128)}) custom-call(s32[1]{0:T(128)} %bitcast.core_ref, f32[16,768]{1,0:T(8,128)} %maximum_maximum_fusion.refs_0_, ...), custom_call_target="tpu_custom_call" | custom-call | flops 1107296256 | bytes 15319040 | tf_op jit(solution)/shard_map/attention_forward/pallas_call | solution.py:124
  28.4 9.9 %feed_forward.2 = (f32[256,768]{1,0:T(8,128)}, bf16[256,768]{1,0:T(8,128)(2,1)}, bf16[256,3072]{1,0:T(8,128)(2,1)}, bf16[256,3072]{1,0:T(8,128)(2,1)}, bf16[256,768]{1,0:T(8,128)(2,1)}) custom-call(s32[1]{0:T(128)} %bitcast.core_ref, f32[16,768]{1,0:T(8,128)} %maximum_maximum_fusion.refs_0_, f32[256,768]{1,0:T(8,128)} %get-tuple-element.52.refs_1_, ...), custom_call_target="tpu_custom_call" | custom-call | flops 2717908992 | bytes 16564224 | tf_op jit(solution)/shard_map/feed_forward/pallas_call | solution.py:124
  40.8 1.6 slice.37
  43.2 1.5 copy.44.refs_3_
  44.7 9.3 %collective-permute-start.1 = (bf16[128,768]{1,0:T(8,128)(2,1)}, bf16[128,768]{1,0:T(8,128)(2,1)S(1)}, u32[]{:S(2)}, u32[]{:S(2)}) collective-permute-start(bf16[128,768]{1,0:T(8,128)(2,1)} %slice.37), channel_id=1, source_target_pairs={{0,1},{2,3},{4,5},{6,7},{8,9},{10,11},{12,13},{14,15},{16,17},{18,... | collective-permute-start | bytes 589832 | tf_op jit(solution)/shard_map/ppermute | solution.py:544
  54.0 1.5 broadcast_select_fusion.6.refs_0_
  55.5 1.5 collective-permute-start.3
  57.0 1.6 slice_select_fusion.refs_5_
  58.6 1.9 copy-done
  60.5 15.6 %attention_forward.3 = (f32[512,768]{1,0:T(8,128)}, bf16[512,768]{1,0:T(8,128)(2,1)}, bf16[3,512,768]{2,1,0:T(8,128)(2,1)}, bf16[512,768]{1,0:T(8,128)(2,1)}, f32[6,8,512]{2,1,0:T(8,128)}, /*index=5*/f32[512,512]{1,0:T(8,128)}) custom-call(s32[1]{0:T(128)} %bitcast.core_ref, f32[16,768]{1,0:T(8,128)} %broadcast_select_fusion.6.refs_0_, ...), custom_call_target="tpu_custom_call" | custom-call | flops 2617245696 | bytes 29712384 | tf_op jit(solution)/shard_map/attention_forward/pallas_call | solution.py:124
  76.1 15.7 %feed_forward.3 = (f32[512,768]{1,0:T(8,128)}, bf16[512,768]{1,0:T(8,128)(2,1)}, bf16[512,3072]{1,0:T(8,128)(2,1)}, bf16[512,3072]{1,0:T(8,128)(2,1)}, bf16[512,768]{1,0:T(8,128)(2,1)}) custom-call(s32[1]{0:T(128)} %bitcast.core_ref, f32[16,768]{1,0:T(8,128)} %broadcast_select_fusion.6.refs_0_, f32[512,768]{1,0:T(8,128)} %get-tuple-element.57.refs_1_, ...), custom_call_target="tpu_custom_call" | custom-call | flops 5435817984 | bytes 33079296 | tf_op jit(solution)/shard_map/feed_forward/pallas_call | solution.py:124
  92.7 22.2 %feed_backward.2 = (bf16[16,5,48,384]{3,2,1,0:T(8,128)(2,1)}, bf16[16,5,48,384]{3,2,1,0:T(8,128)(2,1)}, bf16[16,192,384]{2,1,0:T(8,128)(2,1)}, bf16[16,192,384]{...) custom-call(s32[1]{0:T(128)} %bitcast.core_ref, ...), custom_call_target="tpu_custom_call" | custom-call | flops 10871635968 | bytes 45318144 | tf_op jit(solution)/shard_map/feed_backward/pallas_call | solution.py:124
  114.9 34.4 %attention_backward.2 = (bf16[16,3,48,384]{3,2,1,0:T(8,128)(2,1)}, bf16[16,3,48,384]{3,2,1,0:T(8,128)(2,1)}, f32[16,768]{1,0:T(8,128)}, bf16[128,768]{1,0:T(8,128)(2,1)}) custom-call(s32[1]{0:T(128)} %bitcast.core_ref, f32[16,768]{1,0:T(8,128)} %broadcast_select_fusion.6.refs_0_, f32[512,768]{1,0:T(8,128)} %get-tuple-element.57.refs_1_, ...), custom_call_target="tpu_custom_call" | custom-call | flops 5637144576 | bytes 34131968 | tf_op jit(solution)/shard_map/attention_backward/pallas_call | solution.py:124
  150.6 2.2 collective-permute-done.7
  152.8 1.7 maximum_select_fusion.1.refs_1_
  154.6 14.3 %feed_backward.3 = (bf16[16,5,48,384]{3,2,1,0:T(8,128)(2,1)}, bf16[16,5,48,384]{3,2,1,0:T(8,128)(2,1)}, bf16[16,192,384]{2,1,0:T(8,128)(2,1)}, bf16[16,192,384]{...) custom-call(s32[1]{0:T(128)} %bitcast.core_ref, ...), custom_call_target="tpu_custom_call" | custom-call | flops 5435817984 | bytes 27623424 | tf_op jit(solution)/shard_map/feed_backward/pallas_call | solution.py:124
  168.9 19.7 %attention_backward.3 = (bf16[16,3,48,384]{3,2,1,0:T(8,128)(2,1)}, bf16[16,3,48,384]{3,2,1,0:T(8,128)(2,1)}, f32[16,768]{1,0:T(8,128)}, bf16[2,512,768]{2,1,0:T(8,128)(2,1)}) custom-call(s32[1]{0:T(128)} %bitcast.core_ref, f32[16,768]{1,0:T(8,128)} %maximum_maximum_fusion.refs_0_, f32[256,768]{1,0:T(8,128)} %get-tuple-element.52.refs_1_, ...), custom_call_target="tpu_custom_call" | custom-call | flops 2315255808 | bytes 20127744 | tf_op jit(solution)/shard_map/attention_backward/pallas_call | solution.py:124
  191.5 3.0 collective-permute-start.43
  195.0 2.6 collective-permute-done.43
  198.5 1.8 collective-permute-start.44
  200.3 2.9 collective-permute-done.44
  203.2 1.9 collective-permute-start.45
  205.1 2.8 collective-permute-done.45
  207.9 3.4 collective-permute-start.46
  211.2 2.5 collective-permute-start.8
  217.4 3.1 fusion.8
  220.8 2.1 add_convert_fusion.2
  223.0 2.0 add_convert_fusion.3
  225.5 1.6 collective-permute-start.15
  229.4 2.3 fusion.1
  232.6 1.6 collective-permute-start.37
  234.3 13.7 %collective-permute-done.15 = bf16[2,2,2,144,384]{4,3,0,1,2:T(8,128)(2,1)S(1)} collective-permute-done((bf16[2,2,2,144,384]{4,3,0,1,2:T(8,128)(2,1)S(1)}, bf16[2,2,2,144,384]{4,3,0,1,2:T(8,128)(2,1)S(1)}, u32[]{:S(2)}, u32[]{:S(2)}) %collective-permute-start.15) | collective-permute-done | bytes 884768 | tf_op jit(solution)/shard_map/ppermute | solution.py:560
  248.0 1.5 collective-permute-start.32
  249.8 16.4 %collective-permute-done.10 = bf16[2,2,2,144,384]{4,3,0,1,2:T(8,128)(2,1)S(1)} collective-permute-done((bf16[2,2,2,144,384]{4,3,0,1,2:T(8,128)(2,1)S(1)}, bf16[2,2,2,144,384]{4,3,0,1,2:T(8,128)(2,1)S(1)}, u32[]{:S(2)}, u32[]{:S(2)}) %collective-permute-start.10) | collective-permute-done | bytes 884768 | tf_op jit(solution)/shard_map/ppermute | solution.py:560
  266.2 1.5 collective-permute-start.16
  271.8 1.5 collective-permute-start.26
  276.1 20.2 %collective-permute-done.16 = bf16[2,2,144,384]{3,2,0,1:T(8,128)(2,1)S(1)} collective-permute-done((bf16[2,2,144,384]{3,2,0,1:T(8,128)(2,1)S(1)}, bf16[2,2,144,384]{3,2,0,1:T(8,128)(2,1)S(1)}, u32[]{:S(2)}, u32[]{:S(2)}) %collective-permute-start.16) | collective-permute-done | bytes 442400 | tf_op jit(solution)/shard_map/ppermute | solution.py:560
  296.3 1.5 collective-permute-start.21
  297.9 6.4 %collective-permute-done.11 = bf16[2,2,144,384]{3,2,0,1:T(8,128)(2,1)S(1)} collective-permute-done((bf16[2,2,144,384]{3,2,0,1:T(8,128)(2,1)S(1)}, bf16[2,2,144,384]{3,2,0,1:T(8,128)(2,1)S(1)}, u32[]{:S(2)}, u32[]{:S(2)}) %collective-permute-start.11) | collective-permute-done | bytes 442400 | tf_op jit(solution)/shard_map/ppermute | solution.py:560
  305.2 5.3 %collective-permute-done.17 = bf16[2,144,384]{2,1,0:T(8,128)(2,1)S(1)} collective-permute-done((bf16[2,144,384]{2,1,0:T(8,128)(2,1)S(1)}, bf16[2,144,384]{2,1,0:T(8,128)(2,1)S(1)}, u32[]{:S(2)}, u32[]{:S(2)}) %collective-permute-start.17) | collective-permute-done | bytes 221216 | tf_op jit(solution)/shard_map/ppermute | solution.py:560
  311.3 5.1 %collective-permute-done.12 = bf16[2,144,384]{2,1,0:T(8,128)(2,1)S(1)} collective-permute-done((bf16[2,144,384]{2,1,0:T(8,128)(2,1)S(1)}, bf16[2,144,384]{2,1,0:T(8,128)(2,1)S(1)}, u32[]{:S(2)}, u32[]{:S(2)}) %collective-permute-start.12) | collective-permute-done | bytes 221216 | tf_op jit(solution)/shard_map/ppermute | solution.py:560
  316.5 2.4 collective-permute-start.18
  318.9 4.7 %collective-permute-done.18 = bf16[144,384]{1,0:T(8,128)(2,1)S(1)} collective-permute-done((bf16[144,384]{1,0:T(8,128)(2,1)S(1)}, bf16[144,384]{1,0:T(8,128)(2,1)S(1)}, u32[]{:S(2)}, u32[]{:S(2)}) %collective-permute-start.18) | collective-permute-done | bytes 110624 | tf_op jit(solution)/shard_map/ppermute | solution.py:560
  324.7 4.6 %collective-permute-done.13 = bf16[144,384]{1,0:T(8,128)(2,1)S(1)} collective-permute-done((bf16[144,384]{1,0:T(8,128)(2,1)S(1)}, bf16[144,384]{1,0:T(8,128)(2,1)S(1)}, u32[]{:S(2)}, u32[]{:S(2)}) %collective-permute-start.13) | collective-permute-done | bytes 110624 | tf_op jit(solution)/shard_map/ppermute | solution.py:560
  330.7 1.5 collective-permute-start.38
  335.7 15.8 %collective-permute-done.38 = bf16[2,2,192,384]{3,2,0,1:T(8,128)(2,1)} collective-permute-done((bf16[2,2,192,384]{3,2,0,1:T(8,128)(2,1)}, bf16[2,2,192,384]{3,2,0,1:T(8,128)(2,1)}, u32[]{:S(2)}, u32[]{:S(2)}) %collective-permute-start.38) | collective-permute-done | bytes 589856 | tf_op jit(solution)/shard_map/ppermute | solution.py:560
  351.6 1.4 fusion.11
  353.1 9.2 %collective-permute-done.33 = bf16[2,2,192,384]{3,2,0,1:T(8,128)(2,1)} collective-permute-done((bf16[2,2,192,384]{3,2,0,1:T(8,128)(2,1)}, bf16[2,2,192,384]{3,2,0,1:T(8,128)(2,1)}, u32[]{:S(2)}, u32[]{:S(2)}) %collective-permute-start.33) | collective-permute-done | bytes 589856 | tf_op jit(solution)/shard_map/ppermute | solution.py:560
  364.3 1.7 fusion.2
  367.1 3.1 collective-permute-start.40
  370.2 1.9 fusion.3
  372.2 1.6 collective-permute-start.22
  373.9 1.7 collective-permute-start.35
  375.6 10.0 %collective-permute-done.27 = bf16[2,2,240,384]{3,2,1,0:T(8,128)(2,1)S(1)} collective-permute-done((bf16[2,2,240,384]{3,2,1,0:T(8,128)(2,1)S(1)}, bf16[2,2,240,384]{3,2,1,0:T(8,128)(2,1)S(1)}, u32[]{:S(2)}, u32[]{:S(2)}) %collective-permute-start.27) | collective-permute-done | bytes 737312 | tf_op jit(solution)/shard_map/ppermute | solution.py:560
  385.8 1.4 collective-permute-start.28
  387.3 12.3 %collective-permute-done.22 = bf16[2,2,240,384]{3,2,1,0:T(8,128)(2,1)S(1)} collective-permute-done((bf16[2,2,240,384]{3,2,1,0:T(8,128)(2,1)S(1)}, bf16[2,2,240,384]{3,2,1,0:T(8,128)(2,1)S(1)}, u32[]{:S(2)}, u32[]{:S(2)}) %collective-permute-start.22) | collective-permute-done | bytes 737312 | tf_op jit(solution)/shard_map/ppermute | solution.py:560
  400.5 3.0 collective-permute-start.29
  403.5 9.1 %collective-permute-done.23 = bf16[2,240,384]{2,1,0:T(8,128)(2,1)S(1)} collective-permute-done((bf16[2,240,384]{2,1,0:T(8,128)(2,1)S(1)}, bf16[2,240,384]{2,1,0:T(8,128)(2,1)S(1)}, u32[]{:S(2)}, u32[]{:S(2)}) %collective-permute-start.23) | collective-permute-done | bytes 368672 | tf_op jit(solution)/shard_map/ppermute | solution.py:560
  412.7 1.5 collective-permute-start.24
  414.2 8.0 %collective-permute-done.24 = bf16[240,384]{1,0:T(8,128)(2,1)S(1)} collective-permute-done((bf16[240,384]{1,0:T(8,128)(2,1)S(1)}, bf16[240,384]{1,0:T(8,128)(2,1)S(1)}, u32[]{:S(2)}, u32[]{:S(2)}) %collective-permute-start.24) | collective-permute-done | bytes 184352 | tf_op jit(solution)/shard_map/ppermute | solution.py:560
  (182 shorter events, 52.7 us)
Async XLA Ops:
  0.6 75.4 %collective-permute-start.5 = (bf16[768,3072]{1,0:T(8,128)(2,1)}, bf16[768,3072]{1,0:T(8,128)(2,1)}, u32[]{:S(2)}, u32[]{:S(2)}) collective-permute-start(bf16[768,3072]{1,0:T(8,128)(2,1)} %bitcast.206), channel_id=1, source_target_pairs={{1,0},{3,2},{5,4},{7,6},{9,8},{11,10},{13,12},{15,14},{17,16},{19,... | collective-permute-start | bytes 14155784 | tf_op jit(solution)/shard_map/ppermute | solution.py:544
  1.9 74.2 %collective-permute-start.6 = (bf16[3072,768]{1,0:T(8,128)(2,1)}, bf16[3072,768]{1,0:T(8,128)(2,1)}, u32[]{:S(2)}, u32[]{:S(2)}) collective-permute-start(bf16[3072,768]{1,0:T(8,128)(2,1)} %bitcast.211), channel_id=1, source_target_pairs={{1,0},{3,2},{5,4},{7,6},{9,8},{11,10},{13,12},{15,14},{17,16},{19,... | collective-permute-start | bytes 14155784 | tf_op jit(solution)/shard_map/ppermute | solution.py:544
  3.2 55.4 %collective-permute-start.2 = (bf16[768,2304]{1,0:T(8,128)(2,1)}, bf16[768,2304]{1,0:T(8,128)(2,1)S(1)}, u32[]{:S(2)}, u32[]{:S(2)}) collective-permute-start(bf16[768,2304]{1,0:T(8,128)(2,1)} %bitcast.193), channel_id=1, source_target_pairs={{1,0},{3,2},{5,4},{7,6},{9,8},{11,10},{13,12},{15,14},{17,16},{19,... | collective-permute-start | bytes 10616840 | tf_op jit(solution)/shard_map/ppermute | solution.py:544
  8.6 1.9 copy-start.18
  10.5 34.2 %collective-permute-start = (f32[16,768]{1,0:T(8,128)}, f32[16,768]{1,0:T(8,128)}, u32[]{:S(2)}, u32[]{:S(2)}) collective-permute-start(f32[16,768]{1,0:T(8,128)} %maximum_maximum_fusion.refs_0_), channel_id=1, source_target_pairs={{1,0},{3,2},{5,4},{7,6},{9,8},{11,10},{13,12},{15,14},{17,16},{19,... | collective-permute-start | bytes 147464 | tf_op jit(solution)/shard_map/ppermute | solution.py:544
  11.8 64.3 %collective-permute-start.4 = (bf16[768,768]{1,0:T(8,128)(2,1)}, bf16[768,768]{1,0:T(8,128)(2,1)}, u32[]{:S(2)}, u32[]{:S(2)}) collective-permute-start(bf16[768,768]{1,0:T(8,128)(2,1)} %bitcast.225), channel_id=1, source_target_pairs={{1,0},{3,2},{5,4},{7,6},{9,8},{11,10},{13,12},{15,14},{17,16},{19,... | collective-permute-start | bytes 3538952 | tf_op jit(solution)/shard_map/ppermute | solution.py:544
  28.4 9.9 %copy-start.16 = (s32[2,512]{1,0:T(2,128)S(1)}, s32[2,512]{1,0:T(2,128)}, u32[]{:S(2)}) copy-start(s32[2,512]{1,0:T(2,128)} %param.12) | copy-start | bytes 12292
  28.4 10.5 %copy-start.3 = (bf16[1,2,512,768]{3,2,1,0:T(8,128)(2,1)S(1)}, bf16[1,2,512,768]{3,2,1,0:T(8,128)(2,1)}, u32[]{:S(2)}) copy-start(bf16[1,2,512,768]{3,2,1,0:T(8,128)(2,1)} %param.11) | copy-start | bytes 4718596
  38.3 1.9 copy-start.17
  44.7 10.8 %collective-permute-start.1 = (bf16[128,768]{1,0:T(8,128)(2,1)}, bf16[128,768]{1,0:T(8,128)(2,1)S(1)}, u32[]{:S(2)}, u32[]{:S(2)}) collective-permute-start(bf16[128,768]{1,0:T(8,128)(2,1)} %slice.37), channel_id=1, source_target_pairs={{0,1},{2,3},{4,5},{6,7},{8,9},{10,11},{12,13},{14,15},{16,17},{18,... | collective-permute-start | bytes 589832 | tf_op jit(solution)/shard_map/ppermute | solution.py:544
  55.5 36.3 %collective-permute-start.3 = (bf16[512,768]{1,0:T(8,128)(2,1)}, bf16[512,768]{1,0:T(8,128)(2,1)S(1)}, u32[]{:S(2)}, u32[]{:S(2)}) collective-permute-start(bf16[512,768]{1,0:T(8,128)(2,1)} %get-tuple-element.128), channel_id=1, source_target_pairs={{1,0},{3,2},{5,4},{7,6},{9,8},{11,10},{13,12},{15,14},{17,16},{19,... | collective-permute-start | bytes 2359304 | tf_op jit(solution)/shard_map/ppermute | solution.py:544
  58.6 1.9 copy-start
  149.3 3.5 collective-permute-start.7
  168.9 19.7 %copy-start.14 = (f32[16,768]{1,0:T(8,128)S(1)}, f32[16,768]{1,0:T(8,128)}, u32[]{:S(2)}) copy-start(f32[16,768]{1,0:T(8,128)} %get-tuple-element.94) | copy-start | bytes 147460
  168.9 42.3 %copy-start.13 = (bf16[512,768]{1,0:T(8,128)(2,1)S(1)}, bf16[512,768]{1,0:T(8,128)(2,1)}, u32[]{:S(2)}) copy-start(bf16[512,768]{1,0:T(8,128)(2,1)} %get-tuple-element.81) | copy-start | bytes 2359300
  189.4 1.3 collective-permute-start.42
  189.5 31.0 %collective-permute-start.14 = (bf16[16,3,48,384]{3,2,1,0:T(8,128)(2,1)}, bf16[16,3,48,384]{3,2,1,0:T(8,128)(2,1)}, u32[]{:S(2)}, u32[]{:S(2)}) collective-permute-start(bf16[16,3,48,384]{3,2,1,0:T(8,128)(2,1)} %get-tuple-element.85), channel_id=1, source_target_pairs={{0,1},{1,0},{2,3},{3,2},{4,5},{5,4},{6,7},{7,6},{8,9},{9,8},{10,11... | collective-permute-start | bytes 5308424 | tf_op jit(solution)/shard_map/ppermute | solution.py:544
  191.5 6.1 %collective-permute-start.43 = (f32[2,16,768]{2,1,0:T(8,128)S(1)}, f32[2,16,768]{2,1,0:T(8,128)S(1)}, u32[]{:S(2)}, u32[]{:S(2)}) collective-permute-start(f32[2,16,768]{2,1,0:T(8,128)S(1)} %fusion.26), channel_id=1, source_target_pairs={{0,2},{2,0},{4,6},{6,4},{8,10},{10,8},{12,14},{14,12},{16,18},{18,... | collective-permute-start | bytes 294920 | tf_op jit(solution)/shard_map/ppermute | solution.py:591
  194.5 32.6 %collective-permute-start.36 = (bf16[16,1,192,384]{3,2,0,1:T(8,128)(2,1)}, bf16[16,1,192,384]{3,2,0,1:T(8,128)(2,1)S(1)}, u32[]{:S(2)}, u32[]{:S(2)}) collective-permute-start(bf16[16,1,192,384]{3,2,0,1:T(8,128)(2,1)} %bitcast.73), channel_id=1, source_target_pairs={{0,1},{1,0},{2,3},{3,2},{4,5},{5,4},{6,7},{7,6},{8,9},{9,8},{10,11... | collective-permute-start | bytes 7077896 | tf_op jit(solution)/shard_map/ppermute | solution.py:544
  194.5 28.4 %collective-permute-start.9 = (bf16[16,3,48,384]{3,2,1,0:T(8,128)(2,1)}, bf16[16,3,48,384]{3,2,1,0:T(8,128)(2,1)}, u32[]{:S(2)}, u32[]{:S(2)}) collective-permute-start(bf16[16,3,48,384]{3,2,1,0:T(8,128)(2,1)} %get-tuple-element.83), channel_id=1, source_target_pairs={{0,1},{1,0},{2,3},{3,2},{4,5},{5,4},{6,7},{7,6},{8,9},{9,8},{10,11... | collective-permute-start | bytes 5308424 | tf_op jit(solution)/shard_map/ppermute | solution.py:544
  198.5 4.7 %collective-permute-start.44 = (f32[2,16,768]{2,1,0:T(8,128)S(1)}, f32[2,16,768]{2,1,0:T(8,128)S(1)}, u32[]{:S(2)}, u32[]{:S(2)}) collective-permute-start(f32[2,16,768]{2,1,0:T(8,128)S(1)} %fusion.27), channel_id=1, source_target_pairs={{0,4},{2,6},{4,0},{6,2},{8,12},{10,14},{12,8},{14,10},{16,20},{18,... | collective-permute-start | bytes 294920 | tf_op jit(solution)/shard_map/ppermute | solution.py:591
  203.2 4.7 %collective-permute-start.45 = (f32[2,16,768]{2,1,0:T(8,128)S(1)}, f32[2,16,768]{2,1,0:T(8,128)S(1)}, u32[]{:S(2)}, u32[]{:S(2)}) collective-permute-start(f32[2,16,768]{2,1,0:T(8,128)S(1)} %add.241), channel_id=1, source_target_pairs={{0,8},{2,10},{4,12},{6,14},{8,0},{10,2},{12,4},{14,6},{16,24},{18,... | collective-permute-start | bytes 294920 | tf_op jit(solution)/shard_map/ppermute | solution.py:591
  207.9 7.0 %collective-permute-start.46 = (f32[2,16,768]{2,1,0:T(8,128)S(1)}, f32[2,16,768]{2,1,0:T(8,128)S(1)}, u32[]{:S(2)}, u32[]{:S(2)}) collective-permute-start(f32[2,16,768]{2,1,0:T(8,128)S(1)} %add.242), channel_id=1, source_target_pairs={{0,16},{2,18},{4,20},{6,22},{8,24},{10,26},{12,28},{14,30},{16,0},... | collective-permute-start | bytes 294920 | tf_op jit(solution)/shard_map/ppermute | solution.py:591
  211.2 5.7 %collective-permute-start.8 = (bf16[512,768]{1,0:T(8,128)(2,1)S(1)}, bf16[512,768]{1,0:T(8,128)(2,1)}, u32[]{:S(2)}, u32[]{:S(2)}) collective-permute-start(bf16[512,768]{1,0:T(8,128)(2,1)S(1)} %copy-done.13), channel_id=1, source_target_pairs={{0,1},{2,3},{4,5},{6,7},{8,9},{10,11},{12,13},{14,15},{16,17},{18,... | collective-permute-start | bytes 2359304 | tf_op jit(solution)/shard_map/ppermute | solution.py:544
  214.9 13.5 %collective-permute-start.31 = (bf16[16,1,192,384]{3,2,0,1:T(8,128)(2,1)}, bf16[16,1,192,384]{3,2,0,1:T(8,128)(2,1)}, u32[]{:S(2)}, u32[]{:S(2)}) collective-permute-start(bf16[16,1,192,384]{3,2,0,1:T(8,128)(2,1)} %bitcast.61), channel_id=1, source_target_pairs={{0,1},{1,0},{2,3},{3,2},{4,5},{5,4},{6,7},{7,6},{8,9},{9,8},{10,11... | collective-permute-start | bytes 7077896 | tf_op jit(solution)/shard_map/ppermute | solution.py:544
  216.9 51.2 %collective-permute-start.25 = (bf16[16,5,48,384]{3,2,1,0:T(8,128)(2,1)}, bf16[16,5,48,384]{3,2,1,0:T(8,128)(2,1)S(1)}, u32[]{:S(2)}, u32[]{:S(2)}) collective-permute-start(bf16[16,5,48,384]{3,2,1,0:T(8,128)(2,1)} %get-tuple-element.89), channel_id=1, source_target_pairs={{0,1},{1,0},{2,3},{3,2},{4,5},{5,4},{6,7},{7,6},{8,9},{9,8},{10,11... | collective-permute-start | bytes 8847368 | tf_op jit(solution)/shard_map/ppermute | solution.py:544
  217.4 3.1 copy-start.19
  217.4 3.4 copy-start.11
  220.5 51.3 %collective-permute-start.20 = (bf16[16,5,48,384]{3,2,1,0:T(8,128)(2,1)S(1)}, bf16[16,5,48,384]{3,2,1,0:T(8,128)(2,1)S(1)}, u32[]{:S(2)}, u32[]{:S(2)}) collective-permute-start(bf16[16,5,48,384]{3,2,1,0:T(8,128)(2,1)S(1)} %copy-done.19), channel_id=1, source_target_pairs={{0,1},{1,0},{2,3},{3,2},{4,5},{5,4},{6,7},{7,6},{8,9},{9,8},{10,11... | collective-permute-start | bytes 8847368 | tf_op jit(solution)/shard_map/ppermute | solution.py:544
  220.8 2.1 copy-start.12
  225.4 2.4 copy-start.9
  225.5 22.6 %collective-permute-start.15 = (bf16[2,2,2,144,384]{4,3,0,1,2:T(8,128)(2,1)S(1)}, bf16[2,2,2,144,384]{4,3,0,1,2:T(8,128)(2,1)S(1)}, u32[]{:S(2)}, u32[]{:S(2)}) collective-permute-start(bf16[2,2,2,144,384]{4,3,0,1,2:T(8,128)(2,1)S(1)} %bitcast.241), channel_id=1, source_target_pairs={{0,2},{2,0},{4,6},{6,4},{8,10},{10,8},{12,14},{14,12},{16,18},{18,... | collective-permute-start | bytes 2654216 | tf_op jit(solution)/shard_map/ppermute | solution.py:560
  227.1 39.1 %collective-permute-start.10 = (bf16[2,2,2,144,384]{4,3,0,1,2:T(8,128)(2,1)S(1)}, bf16[2,2,2,144,384]{4,3,0,1,2:T(8,128)(2,1)S(1)}, u32[]{:S(2)}, u32[]{:S(2)}) collective-permute-start(bf16[2,2,2,144,384]{4,3,0,1,2:T(8,128)(2,1)S(1)} %bitcast.240), channel_id=1, source_target_pairs={{0,2},{2,0},{4,6},{6,4},{8,10},{10,8},{12,14},{14,12},{16,18},{18,... | collective-permute-start | bytes 2654216 | tf_op jit(solution)/shard_map/ppermute | solution.py:560
  232.6 96.8 %collective-permute-start.37 = (bf16[2,2,2,192,384]{4,3,0,1,2:T(8,128)(2,1)S(1)}, bf16[2,2,2,192,384]{4,3,0,1,2:T(8,128)(2,1)S(1)}, u32[]{:S(2)}, u32[]{:S(2)}) collective-permute-start(bf16[2,2,2,192,384]{4,3,0,1,2:T(8,128)(2,1)S(1)} %bitcast.239), channel_id=1, source_target_pairs={{0,4},{2,6},{4,0},{6,2},{8,12},{10,14},{12,8},{14,10},{16,20},{18,... | collective-permute-start | bytes 3538952 | tf_op jit(solution)/shard_map/ppermute | solution.py:560
  248.0 84.2 %collective-permute-start.32 = (bf16[2,2,2,192,384]{4,3,0,1,2:T(8,128)(2,1)S(1)}, bf16[2,2,2,192,384]{4,3,0,1,2:T(8,128)(2,1)S(1)}, u32[]{:S(2)}, u32[]{:S(2)}) collective-permute-start(bf16[2,2,2,192,384]{4,3,0,1,2:T(8,128)(2,1)S(1)} %bitcast.238), channel_id=1, source_target_pairs={{0,4},{2,6},{4,0},{6,2},{8,12},{10,14},{12,8},{14,10},{16,20},{18,... | collective-permute-start | bytes 3538952 | tf_op jit(solution)/shard_map/ppermute | solution.py:560
  266.2 30.1 %collective-permute-start.16 = (bf16[2,2,144,384]{3,2,0,1:T(8,128)(2,1)S(1)}, bf16[2,2,144,384]{3,2,0,1:T(8,128)(2,1)S(1)}, u32[]{:S(2)}, u32[]{:S(2)}) collective-permute-start(bf16[2,2,144,384]{3,2,0,1:T(8,128)(2,1)S(1)} %dynamic-slice_bitcast_fusion.6), channel_id=1, source_target_pairs={{0,4},{2,6},{4,0},{6,2},{8,12},{10,14},{12,8},{14,10},{16,20},{18,... | collective-permute-start | bytes 1327112 | tf_op jit(solution)/shard_map/ppermute | solution.py:560
  267.7 1.8 copy-start.7
  268.1 36.3 %collective-permute-start.11 = (bf16[2,2,144,384]{3,2,0,1:T(8,128)(2,1)S(1)}, bf16[2,2,144,384]{3,2,0,1:T(8,128)(2,1)S(1)}, u32[]{:S(2)}, u32[]{:S(2)}) collective-permute-start(bf16[2,2,144,384]{3,2,0,1:T(8,128)(2,1)S(1)} %dynamic-slice_bitcast_fusion.7), channel_id=1, source_target_pairs={{0,4},{2,6},{4,0},{6,2},{8,12},{10,14},{12,8},{14,10},{16,20},{18,... | collective-permute-start | bytes 1327112 | tf_op jit(solution)/shard_map/ppermute | solution.py:560
  270.4 4.3 %copy-start.1 = (bf16[16,5,48,384]{3,2,1,0:T(8,128)(2,1)}, bf16[16,5,48,384]{3,2,1,0:T(8,128)(2,1)S(1)}, u32[]{:S(2)}) copy-start(bf16[16,5,48,384]{3,2,1,0:T(8,128)(2,1)S(1)} %add_convert_fusion) | copy-start | bytes 8847364
  270.5 3.4 copy-start.8
  271.8 92.5 %collective-permute-start.26 = (bf16[2,2,2,240,384]{4,3,2,1,0:T(8,128)(2,1)}, bf16[2,2,2,240,384]{4,3,2,1,0:T(8,128)(2,1)}, u32[]{:S(2)}, u32[]{:S(2)}) collective-permute-start(bf16[2,2,2,240,384]{4,3,2,1,0:T(8,128)(2,1)} %dynamic-slice_bitcast_fusion), channel_id=1, source_target_pairs={{0,2},{2,0},{4,6},{6,4},{8,10},{10,8},{12,14},{14,12},{16,18},{18,... | collective-permute-start | bytes 4423688 | tf_op jit(solution)/shard_map/ppermute | solution.py:560
  296.3 73.9 %collective-permute-start.21 = (bf16[2,2,2,240,384]{4,3,2,1,0:T(8,128)(2,1)}, bf16[2,2,2,240,384]{4,3,2,1,0:T(8,128)(2,1)}, u32[]{:S(2)}, u32[]{:S(2)}) collective-permute-start(bf16[2,2,2,240,384]{4,3,2,1,0:T(8,128)(2,1)} %dynamic-slice_bitcast_fusion.1), channel_id=1, source_target_pairs={{0,2},{2,0},{4,6},{6,4},{8,10},{10,8},{12,14},{14,12},{16,18},{18,... | collective-permute-start | bytes 4423688 | tf_op jit(solution)/shard_map/ppermute | solution.py:560
  304.4 6.2 %collective-permute-start.17 = (bf16[2,144,384]{2,1,0:T(8,128)(2,1)S(1)}, bf16[2,144,384]{2,1,0:T(8,128)(2,1)S(1)}, u32[]{:S(2)}, u32[]{:S(2)}) collective-permute-start(bf16[2,144,384]{2,1,0:T(8,128)(2,1)S(1)} %dynamic-slice_bitcast_fusion.12), channel_id=1, source_target_pairs={{0,8},{2,10},{4,12},{6,14},{8,0},{10,2},{12,4},{14,6},{16,24},{18,... | collective-permute-start | bytes 663560 | tf_op jit(solution)/shard_map/ppermute | solution.py:560
  310.5 5.9 %collective-permute-start.12 = (bf16[2,144,384]{2,1,0:T(8,128)(2,1)S(1)}, bf16[2,144,384]{2,1,0:T(8,128)(2,1)S(1)}, u32[]{:S(2)}, u32[]{:S(2)}) collective-permute-start(bf16[2,144,384]{2,1,0:T(8,128)(2,1)S(1)} %dynamic-slice_bitcast_fusion.13), channel_id=1, source_target_pairs={{0,8},{2,10},{4,12},{6,14},{8,0},{10,2},{12,4},{14,6},{16,24},{18,... | collective-permute-start | bytes 663560 | tf_op jit(solution)/shard_map/ppermute | solution.py:560
  316.5 7.2 %collective-permute-start.18 = (bf16[144,384]{1,0:T(8,128)(2,1)S(1)}, bf16[144,384]{1,0:T(8,128)(2,1)S(1)}, u32[]{:S(2)}, u32[]{:S(2)}) collective-permute-start(bf16[144,384]{1,0:T(8,128)(2,1)S(1)} %dynamic-slice_bitcast_fusion.18), channel_id=1, source_target_pairs={{0,16},{2,18},{4,20},{6,22},{8,24},{10,26},{12,28},{14,30},{16,0},... | collective-permute-start | bytes 331784 | tf_op jit(solution)/shard_map/ppermute | solution.py:560
  323.6 5.6 %collective-permute-start.13 = (bf16[144,384]{1,0:T(8,128)(2,1)S(1)}, bf16[144,384]{1,0:T(8,128)(2,1)S(1)}, u32[]{:S(2)}, u32[]{:S(2)}) collective-permute-start(bf16[144,384]{1,0:T(8,128)(2,1)S(1)} %dynamic-slice_bitcast_fusion.19), channel_id=1, source_target_pairs={{0,16},{2,18},{4,20},{6,22},{8,24},{10,26},{12,28},{14,30},{16,0},... | collective-permute-start | bytes 331784 | tf_op jit(solution)/shard_map/ppermute | solution.py:560
  329.3 4.9 %collective-permute-start.19 = (f32[3,48,384]{2,1,0:T(8,128)S(1)}, f32[3,48,384]{2,1,0:T(8,128)S(1)}, u32[]{:S(2)}, u32[]{:S(2)}) collective-permute-start(f32[3,48,384]{2,1,0:T(8,128)S(1)} %broadcast_select_fusion.5), channel_id=1, source_target_pairs={{0,1},{1,0},{2,3},{3,2},{4,5},{5,4},{6,7},{7,6},{8,9},{9,8},{10,11... | collective-permute-start | bytes 663560 | tf_op jit(solution)/shard_map/ppermute | solution.py:544
  329.7 2.8 copy-start.4
  330.7 20.9 %collective-permute-start.38 = (bf16[2,2,192,384]{3,2,0,1:T(8,128)(2,1)}, bf16[2,2,192,384]{3,2,0,1:T(8,128)(2,1)}, u32[]{:S(2)}, u32[]{:S(2)}) collective-permute-start(bf16[2,2,192,384]{3,2,0,1:T(8,128)(2,1)} %dynamic-slice_bitcast_fusion.4), channel_id=1, source_target_pairs={{0,2},{2,0},{4,6},{6,4},{8,10},{10,8},{12,14},{14,12},{16,18},{18,... | collective-permute-start | bytes 1769480 | tf_op jit(solution)/shard_map/ppermute | solution.py:560
  333.7 28.5 %collective-permute-start.33 = (bf16[2,2,192,384]{3,2,0,1:T(8,128)(2,1)}, bf16[2,2,192,384]{3,2,0,1:T(8,128)(2,1)}, u32[]{:S(2)}, u32[]{:S(2)}) collective-permute-start(bf16[2,2,192,384]{3,2,0,1:T(8,128)(2,1)} %dynamic-slice_bitcast_fusion.5), channel_id=1, source_target_pairs={{0,2},{2,0},{4,6},{6,4},{8,10},{10,8},{12,14},{14,12},{16,18},{18,... | collective-permute-start | bytes 1769480 | tf_op jit(solution)/shard_map/ppermute | solution.py:560
  335.7 26.5 %copy-start.6 = (bf16[2,2,2,192,384]{4,3,0,1,2:T(8,128)(2,1)S(1)}, bf16[2,2,2,192,384]{4,3,0,1,2:T(8,128)(2,1)}, u32[]{:S(2)}) copy-start(bf16[2,2,2,192,384]{4,3,0,1,2:T(8,128)(2,1)} %copy-done.5) | copy-start | bytes 3538948
  353.0 11.3 %copy-start.2 = (bf16[16,5,48,384]{3,2,1,0:T(8,128)(2,1)S(1)}, bf16[16,5,48,384]{3,2,1,0:T(8,128)(2,1)}, u32[]{:S(2)}) copy-start(bf16[16,5,48,384]{3,2,1,0:T(8,128)(2,1)} %copy-done.1) | copy-start | bytes 8847364
  353.0 14.0 %collective-permute-start.39 = (bf16[2,192,384]{2,1,0:T(8,128)(2,1)S(1)}, bf16[2,192,384]{2,1,0:T(8,128)(2,1)S(1)}, u32[]{:S(2)}, u32[]{:S(2)}) collective-permute-start(bf16[2,192,384]{2,1,0:T(8,128)(2,1)S(1)} %dynamic-slice_bitcast_fusion.10), channel_id=1, source_target_pairs={{0,8},{2,10},{4,12},{6,14},{8,0},{10,2},{12,4},{14,6},{16,24},{18,... | collective-permute-start | bytes 884744 | tf_op jit(solution)/shard_map/ppermute | solution.py:560
  363.5 10.3 %collective-permute-start.34 = (bf16[2,192,384]{2,1,0:T(8,128)(2,1)S(1)}, bf16[2,192,384]{2,1,0:T(8,128)(2,1)S(1)}, u32[]{:S(2)}, u32[]{:S(2)}) collective-permute-start(bf16[2,192,384]{2,1,0:T(8,128)(2,1)S(1)} %dynamic-slice_bitcast_fusion.11), channel_id=1, source_target_pairs={{0,8},{2,10},{4,12},{6,14},{8,0},{10,2},{12,4},{14,6},{16,24},{18,... | collective-permute-start | bytes 884744 | tf_op jit(solution)/shard_map/ppermute | solution.py:560
  366.1 19.5 %collective-permute-start.27 = (bf16[2,2,240,384]{3,2,1,0:T(8,128)(2,1)S(1)}, bf16[2,2,240,384]{3,2,1,0:T(8,128)(2,1)S(1)}, u32[]{:S(2)}, u32[]{:S(2)}) collective-permute-start(bf16[2,2,240,384]{3,2,1,0:T(8,128)(2,1)S(1)} %dynamic-slice_bitcast_fusion.2), channel_id=1, source_target_pairs={{0,4},{2,6},{4,0},{6,2},{8,12},{10,14},{12,8},{14,10},{16,20},{18,... | collective-permute-start | bytes 2211848 | tf_op jit(solution)/shard_map/ppermute | solution.py:560
  367.1 33.1 %collective-permute-start.40 = (bf16[192,384]{1,0:T(8,128)(2,1)S(1)}, bf16[192,384]{1,0:T(8,128)(2,1)S(1)}, u32[]{:S(2)}, u32[]{:S(2)}) collective-permute-start(bf16[192,384]{1,0:T(8,128)(2,1)S(1)} %dynamic-slice_bitcast_fusion.16), channel_id=1, source_target_pairs={{0,16},{2,18},{4,20},{6,22},{8,24},{10,26},{12,28},{14,30},{16,0},... | collective-permute-start | bytes 442376 | tf_op jit(solution)/shard_map/ppermute | solution.py:560
  372.2 27.3 %collective-permute-start.22 = (bf16[2,2,240,384]{3,2,1,0:T(8,128)(2,1)S(1)}, bf16[2,2,240,384]{3,2,1,0:T(8,128)(2,1)S(1)}, u32[]{:S(2)}, u32[]{:S(2)}) collective-permute-start(bf16[2,2,240,384]{3,2,1,0:T(8,128)(2,1)S(1)} %dynamic-slice_bitcast_fusion.3), channel_id=1, source_target_pairs={{0,4},{2,6},{4,0},{6,2},{8,12},{10,14},{12,8},{14,10},{16,20},{18,... | collective-permute-start | bytes 2211848 | tf_op jit(solution)/shard_map/ppermute | solution.py:560
  373.9 26.2 %collective-permute-start.35 = (bf16[192,384]{1,0:T(8,128)(2,1)S(1)}, bf16[192,384]{1,0:T(8,128)(2,1)S(1)}, u32[]{:S(2)}, u32[]{:S(2)}) collective-permute-start(bf16[192,384]{1,0:T(8,128)(2,1)S(1)} %dynamic-slice_bitcast_fusion.17), channel_id=1, source_target_pairs={{0,16},{2,18},{4,20},{6,22},{8,24},{10,26},{12,28},{14,30},{16,0},... | collective-permute-start | bytes 442376 | tf_op jit(solution)/shard_map/ppermute | solution.py:560
  385.8 14.5 %collective-permute-start.28 = (bf16[2,240,384]{2,1,0:T(8,128)(2,1)S(1)}, bf16[2,240,384]{2,1,0:T(8,128)(2,1)S(1)}, u32[]{:S(2)}, u32[]{:S(2)}) collective-permute-start(bf16[2,240,384]{2,1,0:T(8,128)(2,1)S(1)} %dynamic-slice_bitcast_fusion.8), channel_id=1, source_target_pairs={{0,8},{2,10},{4,12},{6,14},{8,0},{10,2},{12,4},{14,6},{16,24},{18,... | collective-permute-start | bytes 1105928 | tf_op jit(solution)/shard_map/ppermute | solution.py:560
  399.8 12.8 %collective-permute-start.23 = (bf16[2,240,384]{2,1,0:T(8,128)(2,1)S(1)}, bf16[2,240,384]{2,1,0:T(8,128)(2,1)S(1)}, u32[]{:S(2)}, u32[]{:S(2)}) collective-permute-start(bf16[2,240,384]{2,1,0:T(8,128)(2,1)S(1)} %dynamic-slice_bitcast_fusion.9), channel_id=1, source_target_pairs={{0,8},{2,10},{4,12},{6,14},{8,0},{10,2},{12,4},{14,6},{16,24},{18,... | collective-permute-start | bytes 1105928 | tf_op jit(solution)/shard_map/ppermute | solution.py:560
  400.3 22.2 %collective-permute-start.41 = (f32[1,192,384]{2,1,0:T(8,128)S(1)}, f32[1,192,384]{2,1,0:T(8,128)S(1)}, u32[]{:S(2)}, u32[]{:S(2)}) collective-permute-start(f32[1,192,384]{2,1,0:T(8,128)S(1)} %select_bitcast_fusion), channel_id=1, source_target_pairs={{0,1},{1,0},{2,3},{3,2},{4,5},{5,4},{6,7},{7,6},{8,9},{9,8},{10,11... | collective-permute-start | bytes 884744 | tf_op jit(solution)/shard_map/ppermute | solution.py:544
  400.5 13.7 %collective-permute-start.29 = (bf16[240,384]{1,0:T(8,128)(2,1)S(1)}, bf16[240,384]{1,0:T(8,128)(2,1)S(1)}, u32[]{:S(2)}, u32[]{:S(2)}) collective-permute-start(bf16[240,384]{1,0:T(8,128)(2,1)S(1)} %dynamic-slice_bitcast_fusion.14), channel_id=1, source_target_pairs={{0,16},{2,18},{4,20},{6,22},{8,24},{10,26},{12,28},{14,30},{16,0},... | collective-permute-start | bytes 552968 | tf_op jit(solution)/shard_map/ppermute | solution.py:560
  412.7 9.5 %collective-permute-start.24 = (bf16[240,384]{1,0:T(8,128)(2,1)S(1)}, bf16[240,384]{1,0:T(8,128)(2,1)S(1)}, u32[]{:S(2)}, u32[]{:S(2)}) collective-permute-start(bf16[240,384]{1,0:T(8,128)(2,1)S(1)} %dynamic-slice_bitcast_fusion.15), channel_id=1, source_target_pairs={{0,16},{2,18},{4,20},{6,22},{8,24},{10,26},{12,28},{14,30},{16,0},... | collective-permute-start | bytes 552968 | tf_op jit(solution)/shard_map/ppermute | solution.py:560
  422.3 1.8 collective-permute-start.30
  (4 other events, 4.4 us)
